TPU v7x, 128 devices: a whole 4x4x4 slice. The times are simulated.
128 devices in a mesh: dp: 16 (over y_lo, x, core), tensor: 8 (over y_hi, z).
Axes of the slice: x: 4, y: 4 (y_hi: 2, y_lo: 2; y = y_hi * 2 + y_lo), z: 4, core: 2. Of those that a mesh axis runs over, the one named last changes fastest.
Arguments:
- tokens: bfloat16 [32768, 1152], P(('dp', 'tensor')), may hold values from -6 to 6
- picture: int32 [32768], P('dp'), may hold values from -1 to 10, as said below
- cotangent: bfloat16 [32768, 1152], P(('dp', 'tensor')), may hold values from -6 to 6
- gain_one: bfloat16 [1152], replicated, may hold values from 0.5 to 1.5
- shift_one: bfloat16 [1152], replicated, may hold values from -0.625 to 0.625
- query_weight: bfloat16 [1152, 1152], P('dp', 'tensor'), may hold values from -0.1875 to 0.1875
- query_bias: bfloat16 [1152], replicated, may hold values from -1.75 to 1.75
- key_weight: bfloat16 [1152, 1152], P('dp', 'tensor'), may hold values from -0.1875 to 0.1875
- value_weight: bfloat16 [1152, 1152], P('dp', 'tensor'), may hold values from -0.1875 to 0.1875
- value_bias: bfloat16 [1152], replicated, may hold values from -0.3125 to 0.3125
- out_weight: bfloat16 [1152, 1152], P('tensor', 'dp'), may hold values from -1 to 1
- out_bias: bfloat16 [1152], replicated, may hold values from -0.625 to 0.625
- gain_two: bfloat16 [1152], replicated, may hold values from 0.5 to 1.5
- shift_two: bfloat16 [1152], replicated, may hold values from -0.625 to 0.625
- up_weight: bfloat16 [1152, 4304], P('dp', 'tensor'), may hold values from -0.1875 to 0.1875
- up_bias: bfloat16 [4304], replicated, may hold values from -0.625 to 0.625
- down_weight: bfloat16 [4304, 1152], P('tensor', 'dp'), may hold values from -0.09375 to 0.09375
- down_bias: bfloat16 [1152], replicated, may hold values from -0.625 to 0.625
Outputs:
- result: float32 [32768, 1152], P(('dp', 'tensor'))
- grad_tokens: float32 [32768, 1152], P(('dp', 'tensor'))
- grad_query_weight: float32 [1152, 1152], P('dp', 'tensor')
- grad_key_weight: float32 [1152, 1152], P('dp', 'tensor')
- grad_value_weight: float32 [1152, 1152], P('dp', 'tensor')
- grad_out_weight: float32 [1152, 1152], P('tensor', 'dp')
- grad_up_weight: float32 [1152, 4304], P('dp', 'tensor')
- grad_down_weight: float32 [4304, 1152], P('tensor', 'dp')
- grad_query_bias: float32 [1152], replicated
- grad_value_bias: float32 [1152], replicated
- grad_up_bias: float32 [4304], replicated
- grad_out_bias: float32 [1152], replicated
- grad_down_bias: float32 [1152], replicated
- grad_gain_one: float32 [1152], replicated
- grad_shift_one: float32 [1152], replicated
- grad_gain_two: float32 [1152], replicated
- grad_shift_two: float32 [1152], replicated
- clipped_query_weight: float32 [1152, 1152], P('dp', 'tensor')
- clipped_key_weight: float32 [1152, 1152], P('dp', 'tensor')
Inputs may be any that keep to these rules, and one draw needn't show every extreme that they name: Each packed row of 2048 slots holds whole pictures, contiguous runs of 100 to 1024 slots numbered 0, 1, 2, ... from the row's start, followed by padding marked -1 up to the row's end; the first picture of every row has exactly 1024 slots, and the last slot of every row is padding. Some row holds as many pictures as fit.
All inputs are finite; a program needn't handle non-finite values.
Results may differ from a plain program's by a relative error of at most 0.02.
Values may be sent and summed in bfloat16 or wider, within the bound.
A program may use at most 128 MiB of HBM per device.

v0:
```python
import jax
import jax.numpy as jnp
from jax import lax
from jax.sharding import PartitionSpec as P

HEAD_DIM = 72


EPSILON = 1e-06
CLIP_LIMIT = 2.0


def normalize(values, gain, shift):
    centre = values - jnp.mean(values, axis=-1, keepdims=True)
    inverse = lax.rsqrt(jnp.mean(centre * centre, axis=-1, keepdims=True) + EPSILON)
    scaled = centre * inverse
    return (scaled * gain + shift, scaled, inverse)


def normalize_back(upstream, scaled, inverse, gain):
    along = upstream * gain
    width_mean = jnp.mean(along, axis=-1, keepdims=True)
    cross_mean = jnp.mean(along * scaled, axis=-1, keepdims=True)
    return inverse * (along - width_mean - scaled * cross_mean)


def contract_rows(left, right):
    return lax.dot_general(
        left, right, (((0,), (0,)), ((), ())), preferred_element_type=jnp.float32
    )


def contract_cols(left, right):
    return lax.dot_general(
        left, right, (((1,), (1,)), ((), ())), preferred_element_type=jnp.float32
    )


def smooth(inner):
    return jax.nn.gelu(inner, approximate=True)


def padded(vector, total, offset):
    return lax.dynamic_update_slice_in_dim(jnp.zeros((total,), jnp.float32), vector, offset, 0)


def per_device(
    tokens,
    picture,
    cotangent,
    gain_one,
    shift_one,
    query_weight,
    query_bias,
    key_weight,
    value_weight,
    value_bias,
    out_weight,
    out_bias,
    gain_two,
    shift_two,
    up_weight,
    up_bias,
    down_weight,
    down_bias,
):
    width = tokens.shape[1]
    tensor_rank = lax.axis_index("tensor")
    head_cols = query_weight.shape[1]
    heads_local = head_cols // HEAD_DIM
    hidden_cols = up_weight.shape[1]
    hidden_total = up_bias.shape[0]
    row_length = picture.shape[0]
    block_rows = min(512, row_length)
    blocks = row_length // block_rows
    score_scale = HEAD_DIM ** (-0.5)
    gain_first = gain_one.astype(jnp.float32)
    gain_second = gain_two.astype(jnp.float32)
    query_shift = lax.dynamic_slice_in_dim(
        query_bias.astype(jnp.float32), tensor_rank * head_cols, head_cols
    )
    value_shift = lax.dynamic_slice_in_dim(
        value_bias.astype(jnp.float32), tensor_rank * head_cols, head_cols
    )
    up_shift = lax.dynamic_slice_in_dim(
        up_bias.astype(jnp.float32), tensor_rank * hidden_cols, hidden_cols
    )
    positions = jnp.arange(row_length, dtype=jnp.int32)
    block_ids = picture.reshape(blocks, block_rows)
    block_pos = positions.reshape(blocks, block_rows)
    query_full, key_full, value_full, up_full, out_full, down_full = (
        lax.all_gather(query_weight, "dp", axis=0, tiled=True),
        lax.all_gather(key_weight, "dp", axis=0, tiled=True),
        lax.all_gather(value_weight, "dp", axis=0, tiled=True),
        lax.all_gather(up_weight, "dp", axis=0, tiled=True),
        lax.all_gather(out_weight, "dp", axis=1, tiled=True),
        lax.all_gather(down_weight, "dp", axis=1, tiled=True),
    )
    inputs = tokens.astype(jnp.float32)
    normed, scaled_one, inverse_one = normalize(inputs, gain_first, shift_one.astype(jnp.float32))
    rows_one = lax.all_gather(normed.astype(jnp.bfloat16), "tensor", axis=0, tiled=True)
    queries = (
        jnp.dot(rows_one, query_full, preferred_element_type=jnp.float32) + query_shift
    ).astype(jnp.bfloat16)
    keys_all = jnp.dot(rows_one, key_full, preferred_element_type=jnp.float32).astype(jnp.bfloat16)
    values_all = (
        jnp.dot(rows_one, value_full, preferred_element_type=jnp.float32) + value_shift
    ).astype(jnp.bfloat16)
    query_heads = queries.reshape(blocks, block_rows, heads_local, HEAD_DIM)
    keys_heads = keys_all.reshape(row_length, heads_local, HEAD_DIM)
    values_heads = values_all.reshape(row_length, heads_local, HEAD_DIM)

    def block_scores(query_block, query_ids, query_pos):
        scores = (
            jnp.einsum("qhd,khd->hqk", query_block, keys_heads, preferred_element_type=jnp.float32)
            * score_scale
        )
        allowed = (query_ids[:, None] == picture[None, :]) & (query_ids[:, None] >= 0) | (
            query_pos[:, None] == positions[None, :]
        )
        return (scores, allowed)

    def forward_block(pieces):
        query_block, query_ids, query_pos = pieces
        scores, allowed = block_scores(query_block, query_ids, query_pos)
        masked = jnp.where(allowed[None], scores, -1e30)
        top = jnp.max(masked, axis=-1, keepdims=True)
        expo = jnp.exp(masked - top)
        total = jnp.sum(expo, axis=-1, keepdims=True)
        weights = (expo / total).astype(jnp.bfloat16)
        mixed_block = jnp.einsum(
            "hqk,khd->qhd", weights, values_heads, preferred_element_type=jnp.float32
        )
        logsum = (top + jnp.log(total))[..., 0]
        real = allowed & (query_ids[:, None] >= 0)
        peak = jnp.max(jnp.where(real[None], scores, -1e30), axis=(1, 2))
        return (mixed_block.astype(jnp.bfloat16), logsum, peak)

    mixed, logsums, peaks = lax.map(forward_block, (query_heads, block_ids, block_pos))
    mixed = mixed.reshape(row_length, head_cols)
    branch = lax.psum_scatter(
        jnp.dot(mixed, out_full, preferred_element_type=jnp.float32),
        "tensor",
        scatter_dimension=0,
        tiled=True,
    ) + out_bias.astype(jnp.float32)
    middle = inputs + branch
    normed_two, scaled_two, inverse_two = normalize(
        middle, gain_second, shift_two.astype(jnp.float32)
    )
    rows_two = lax.all_gather(normed_two.astype(jnp.bfloat16), "tensor", axis=0, tiled=True)
    hidden = jnp.dot(rows_two, up_full, preferred_element_type=jnp.float32) + up_shift
    active = smooth(hidden).astype(jnp.bfloat16)
    result = middle + (
        lax.psum_scatter(
            jnp.dot(active, down_full, preferred_element_type=jnp.float32).astype(jnp.bfloat16),
            "tensor",
            scatter_dimension=0,
            tiled=True,
        ).astype(jnp.float32)
        + down_bias.astype(jnp.float32)
    )
    global_peak = lax.pmax(jnp.max(peaks, axis=0), "dp")
    factor = jnp.sqrt(CLIP_LIMIT / jnp.maximum(global_peak, CLIP_LIMIT))
    column_factor = jnp.repeat(factor, HEAD_DIM)
    clipped_query = query_weight.astype(jnp.float32) * column_factor[None, :]
    clipped_key = key_weight.astype(jnp.float32) * column_factor[None, :]
    query_back, key_back, value_back, up_back, out_back, down_back = (
        lax.all_gather(query_weight, "dp", axis=0, tiled=True),
        lax.all_gather(key_weight, "dp", axis=0, tiled=True),
        lax.all_gather(value_weight, "dp", axis=0, tiled=True),
        lax.all_gather(up_weight, "dp", axis=0, tiled=True),
        lax.all_gather(out_weight, "dp", axis=1, tiled=True),
        lax.all_gather(down_weight, "dp", axis=1, tiled=True),
    )
    upstream = cotangent.astype(jnp.float32)
    grad_rows = lax.all_gather(cotangent, "tensor", axis=0, tiled=True)
    down_grad = contract_rows(active, grad_rows)
    active_grad = contract_cols(grad_rows, down_back)
    _, gelu_back = jax.vjp(smooth, hidden)
    hidden_grad = gelu_back(active_grad)[0].astype(jnp.bfloat16)
    up_bias_grad = jnp.sum(hidden_grad.astype(jnp.float32), axis=0)
    up_grad = contract_rows(rows_two, hidden_grad)
    normed_two_grad = lax.psum_scatter(
        contract_cols(hidden_grad, up_back), "tensor", scatter_dimension=0, tiled=True
    )
    gain_two_grad = jnp.sum(normed_two_grad * scaled_two, axis=0)
    shift_two_grad = jnp.sum(normed_two_grad, axis=0)
    middle_grad = upstream + normalize_back(normed_two_grad, scaled_two, inverse_two, gain_second)
    down_bias_grad = jnp.sum(upstream, axis=0)
    branch_low = middle_grad.astype(jnp.bfloat16)
    out_bias_grad = jnp.sum(branch_low.astype(jnp.float32), axis=0)
    branch_rows = lax.all_gather(branch_low, "tensor", axis=0, tiled=True)
    out_grad = contract_rows(mixed, branch_rows)
    mixed_grad = contract_cols(branch_rows, out_back).astype(jnp.bfloat16)

    def backward_block(carry, pieces):
        key_sum, value_sum = carry
        query_block, grad_block, logsum, query_ids, query_pos = pieces
        scores, allowed = block_scores(query_block, query_ids, query_pos)
        probs = jnp.where(allowed[None], jnp.exp(scores - logsum[..., None]), 0.0)
        value_sum = value_sum + jnp.einsum(
            "hqk,qhd->khd",
            probs.astype(jnp.bfloat16),
            grad_block,
            preferred_element_type=jnp.float32,
        )
        prob_grad = jnp.einsum(
            "qhd,khd->hqk", grad_block, values_heads, preferred_element_type=jnp.float32
        )
        centre = jnp.sum(probs * prob_grad, axis=-1, keepdims=True)
        score_grad = (probs * (prob_grad - centre)).astype(jnp.bfloat16)
        query_part = (
            jnp.einsum("hqk,khd->qhd", score_grad, keys_heads, preferred_element_type=jnp.float32)
            * score_scale
        )
        key_sum = (
            key_sum
            + jnp.einsum(
                "hqk,qhd->khd", score_grad, query_block, preferred_element_type=jnp.float32
            )
            * score_scale
        )
        return ((key_sum, value_sum), query_part.astype(jnp.bfloat16))

    empty = jnp.zeros((row_length, heads_local, HEAD_DIM), jnp.float32)
    (key_sum, value_sum), query_grad = lax.scan(
        backward_block,
        (empty, empty),
        (
            query_heads,
            mixed_grad.reshape(blocks, block_rows, heads_local, HEAD_DIM),
            logsums,
            block_ids,
            block_pos,
        ),
    )
    query_grad = query_grad.reshape(row_length, head_cols)
    key_grad = key_sum.reshape(row_length, head_cols).astype(jnp.bfloat16)
    value_grad = value_sum.reshape(row_length, head_cols).astype(jnp.bfloat16)
    query_bias_grad = jnp.sum(query_grad.astype(jnp.float32), axis=0)
    value_bias_grad = jnp.sum(value_grad.astype(jnp.float32), axis=0)
    query_w_grad = contract_rows(rows_one, query_grad)
    key_w_grad = contract_rows(rows_one, key_grad)
    value_w_grad = contract_rows(rows_one, value_grad)
    part_query = contract_cols(query_grad, query_back)
    part_key = contract_cols(key_grad, key_back)
    part_value = contract_cols(value_grad, value_back)
    normed_one_grad = lax.psum_scatter(
        (part_query + part_key + part_value).astype(jnp.bfloat16),
        "tensor",
        scatter_dimension=0,
        tiled=True,
    ).astype(jnp.float32)
    gain_one_grad = jnp.sum(normed_one_grad * scaled_one, axis=0)
    shift_one_grad = jnp.sum(normed_one_grad, axis=0)
    input_grad = middle_grad + normalize_back(normed_one_grad, scaled_one, inverse_one, gain_first)
    query_w_part, key_w_part, value_w_part, up_part, out_part, down_part = (
        lax.psum_scatter(
            query_w_grad.astype(jnp.bfloat16), "dp", scatter_dimension=0, tiled=True
        ).astype(jnp.float32),
        lax.psum_scatter(
            key_w_grad.astype(jnp.bfloat16), "dp", scatter_dimension=0, tiled=True
        ).astype(jnp.float32),
        lax.psum_scatter(
            value_w_grad.astype(jnp.bfloat16), "dp", scatter_dimension=0, tiled=True
        ).astype(jnp.float32),
        lax.psum_scatter(
            up_grad.astype(jnp.bfloat16), "dp", scatter_dimension=0, tiled=True
        ).astype(jnp.float32),
        lax.psum_scatter(
            out_grad.astype(jnp.bfloat16), "dp", scatter_dimension=1, tiled=True
        ).astype(jnp.float32),
        lax.psum_scatter(
            down_grad.astype(jnp.bfloat16), "dp", scatter_dimension=1, tiled=True
        ).astype(jnp.float32),
    )
    sums = lax.psum(
        (
            padded(query_bias_grad, width, tensor_rank * head_cols),
            padded(value_bias_grad, width, tensor_rank * head_cols),
            padded(up_bias_grad, hidden_total, tensor_rank * hidden_cols),
            out_bias_grad,
            down_bias_grad,
            gain_one_grad,
            shift_one_grad,
            gain_two_grad,
            shift_two_grad,
        ),
        ("dp", "tensor"),
    )
    return (
        result,
        input_grad,
        query_w_part,
        key_w_part,
        value_w_part,
        out_part,
        up_part,
        down_part,
        sums[0],
        sums[1],
        sums[2],
        sums[3],
        sums[4],
        sums[5],
        sums[6],
        sums[7],
        sums[8],
        clipped_query,
        clipped_key,
    )


def solution(mesh):
    in_specs = (
        P(("dp", "tensor"), None),
        P("dp"),
        P(("dp", "tensor"), None),
        P(),
        P(),
        P("dp", "tensor"),
        P(),
        P("dp", "tensor"),
        P("dp", "tensor"),
        P(),
        P("tensor", "dp"),
        P(),
        P(),
        P(),
        P("dp", "tensor"),
        P(),
        P("tensor", "dp"),
        P(),
    )
    out_specs = (
        P(("dp", "tensor"), None),
        P(("dp", "tensor"), None),
        P("dp", "tensor"),
        P("dp", "tensor"),
        P("dp", "tensor"),
        P("tensor", "dp"),
        P("dp", "tensor"),
        P("tensor", "dp"),
        P(),
        P(),
        P(),
        P(),
        P(),
        P(),
        P(),
        P(),
        P(),
        P("dp", "tensor"),
        P("dp", "tensor"),
    )
    return jax.shard_map(
        per_device, mesh=mesh, in_specs=in_specs, out_specs=out_specs, check_vma=False
    )
```

profile of v0, /device:TPU:1, one launch (start us, length us, event | category | flops | bytes accessed | tf_op | source)
XLA Modules:
  0.0 1264.0 jit_solution(5797799928640252356)
XLA Ops:
  18.6 22.8 %all_gather.40 = bf16[144,1152]{0,1:T(8,128)(2,1)S(1)} all-gather(bf16[144,72]{0,1:T(8,128)(2,1)S(1)} %copy.47), channel_id=1, replica_groups=mesh['dp'=16,'tensor'=8] {'dp'}, dimensions={1}, use_global_device_ids=true | all-gather | bytes 352512 | tf_op jit(solution)/shard_map/all_gather | solution.py:96
  41.5 18.2 %all_gather.39 = bf16[1152,144]{1,0:T(8,128)(2,1)S(1)} all-gather(bf16[72,144]{1,0:T(8,128)(2,1)} %param.30), channel_id=1, replica_groups=mesh['dp'=16,'tensor'=8] {'dp'}, dimensions={0}, use_global_device_ids=true | all-gather | bytes 352512 | tf_op jit(solution)/shard_map/all_gather | solution.py:94
  59.7 19.4 %all_gather.37 = bf16[1152,144]{1,0:T(8,128)(2,1)S(1)} all-gather(bf16[72,144]{1,0:T(8,128)(2,1)S(1)} %copy-done.19), channel_id=1, replica_groups=mesh['dp'=16,'tensor'=8] {'dp'}, dimensions={0}, use_global_device_ids=true | all-gather | bytes 352512 | tf_op jit(solution)/shard_map/all_gather | solution.py:92
  79.0 17.9 %all_gather.38 = bf16[1152,144]{1,0:T(8,128)(2,1)S(1)} all-gather(bf16[72,144]{1,0:T(8,128)(2,1)S(1)} %copy-done.21), channel_id=1, replica_groups=mesh['dp'=16,'tensor'=8] {'dp'}, dimensions={0}, use_global_device_ids=true | all-gather | bytes 352512 | tf_op jit(solution)/shard_map/all_gather | solution.py:93
  110.3 49.7 %while.30 = (s32[]{:T(128)}, bf16[4,512,2,72]{1,3,2,0:T(8,128)(2,1)S(1)}, f32[4,2,512]{2,1,0:T(2,128)}, f32[4,2]{1,0:T(4,128)}, s32[4,512]{1,0:T(4,128)S(1)}, /*...) while((s32[]{:T(128)}, ...), condition=%wide.region_6.7_spmd.clone, body=%wide.region_2.6_spmd.clone.sunk | while | flops 638656000 | bytes 32988328 | solution.py:139
  168.0 122.4 %reduce-scatter.19.cloned.1.call-done = f32[256,1152]{1,0:T(8,128)} async-done(((f32[2048,1152]{1,0:T(8,128)}), f32[256,1152]{1,0:T(8,128)}) %reduce-scatter.19.cloned.1.call-update) | async-done | bytes 1179664 | tf_op jit(solution)/shard_map/reduce_scatter | solution.py:141
  296.2 71.4 %all-gather.9.cloned.1.call-done = bf16[2048,1152]{1,0:T(8,128)(2,1)} async-done(((bf16[256,1152]{1,0:T(8,128)(2,1)}), bf16[2048,1152]{1,0:T(8,128)(2,1)}) %all-gather.9.cloned.1.call-update) | async-done | bytes 4718608 | tf_op jit(solution)/shard_map/all_gather | solution.py:151
  367.6 8.0 fusion.76
  375.6 25.4 %all-gather.13.cloned.1.call-done = bf16[538,1152]{0,1:T(8,128)(2,1)} async-done(((bf16[538,72]{0,1:T(8,128)(2,1)}), bf16[538,1152]{0,1:T(8,128)(2,1)}) %all-gather.13.cloned.1.call-update) | async-done | bytes 1239568 | tf_op jit(solution)/shard_map/all_gather | solution.py:97
  401.1 77.2 %all-gather.15.cloned.1.call-done = bf16[2048,1152]{1,0:T(8,128)(2,1)} async-done(((bf16[256,1152]{1,0:T(8,128)(2,1)}), bf16[2048,1152]{1,0:T(8,128)(2,1)}) %all-gather.15.cloned.1.call-update) | async-done | bytes 4718608 | tf_op jit(solution)/shard_map/all_gather | solution.py:177
  478.3 9.6 convert_reduce_fusion
  496.3 9.8 convolution_convert_fusion
  507.6 110.0 %reduce-scatter.23.cloned.1.call-done = f32[256,1152]{1,0:T(8,128)} async-done(((f32[2048,1152]{1,0:T(8,128)}), f32[256,1152]{1,0:T(8,128)}) %reduce-scatter.23.cloned.1.call-update) | async-done | bytes 1179664 | tf_op jit(solution)/shard_map/reduce_scatter | solution.py:184
  620.6 86.1 %reduce-scatter.21.cloned.1.call-done = bf16[256,1152]{1,0:T(8,128)(2,1)} async-done(((bf16[2048,1152]{1,0:T(8,128)(2,1)}), bf16[256,1152]{1,0:T(8,128)(2,1)}) %reduce-scatter.21.cloned.1.call-update) | async-done | bytes 589840 | tf_op jit(solution)/shard_map/reduce_scatter | solution.py:155
  711.2 9.1 convolution_convert_fusion.1
  720.5 8.5 convolution_convert_fusion.2
  729.1 62.5 %all-gather.17.cloned.1.call-done = bf16[2048,1152]{1,0:T(8,128)(2,1)} async-done(((bf16[256,1152]{1,0:T(8,128)(2,1)}), bf16[2048,1152]{1,0:T(8,128)(2,1)}) %all-gather.17.cloned.1.call-update) | async-done | bytes 4718608 | tf_op jit(solution)/shard_map/all_gather | solution.py:193
  807.7 59.3 %while.31 = (s32[]{:T(128)}, f32[2048,2,72]{0,2,1:T(8,128)S(1)}, f32[2048,2,72]{0,2,1:T(8,128)}, bf16[4,512,2,72]{1,3,2,0:T(8,128)(2,1)S(1)}, bf16[4,512,2,72]{1...) while((s32[]{:T(128)}, f32[2048,2,72]{0,2,1:T(8,128)S(1)}, ...), condition=%wide.region_16.17_spmd.clone, body=%wide.region_14.16_spmd.clone.sunk | while | flops 1547222528 | bytes 86183176 | solution.py:227
  898.6 27.6 %pmax.7 = f32[2]{0:T(128)S(1)} all-reduce(f32[2]{0:T(128)S(1)} %reduce_max.27), channel_id=1, replica_groups=mesh['dp'=16,'tensor'=8] {'dp'}, use_global_device_ids=true, to_apply=%region_45.46 | all-reduce | flops 2 | bytes 16 | tf_op jit(solution)/shard_map/pmax | solution.py:163
  932.8 35.0 %reduce-scatter.27.cloned.1.call-done = bf16[72,144]{1,0:T(8,128)(2,1)} async-done(((bf16[1152,144]{1,0:T(8,128)(2,1)}), bf16[72,144]{1,0:T(8,128)(2,1)}) %reduce-scatter.27.cloned.1.call-update) | async-done | bytes 20752 | tf_op jit(solution)/shard_map/reduce_scatter | solution.py:259
  969.3 60.1 %reduce-scatter.29.cloned.1.call-done = bf16[72,144]{1,0:T(8,128)(2,1)} async-done(((bf16[1152,144]{1,0:T(8,128)(2,1)}), bf16[72,144]{1,0:T(8,128)(2,1)}) %reduce-scatter.29.cloned.1.call-update) | async-done | bytes 20752 | tf_op jit(solution)/shard_map/reduce_scatter | solution.py:262
  1030.8 60.3 %reduce-scatter.31.cloned.1.call-done = bf16[72,144]{1,0:T(8,128)(2,1)} async-done(((bf16[1152,144]{1,0:T(8,128)(2,1)}), bf16[72,144]{1,0:T(8,128)(2,1)}) %reduce-scatter.31.cloned.1.call-update) | async-done | bytes 20752 | tf_op jit(solution)/shard_map/reduce_scatter | solution.py:265
  1092.5 91.2 %reduce-scatter.25.cloned.1.call-done = bf16[256,1152]{1,0:T(8,128)(2,1)} async-done(((bf16[2048,1152]{1,0:T(8,128)(2,1)}), bf16[256,1152]{1,0:T(8,128)(2,1)}) %reduce-scatter.25.cloned.1.call-update) | async-done | bytes 589840 | tf_op jit(solution)/shard_map/reduce_scatter | solution.py:249
  1185.4 68.2 %all-reduce.2 = (f32[1152]{0:T(1024)}, f32[1152]{0:T(1024)}, f32[4304]{0:T(1024)}, f32[1152]{0:T(1024)}, f32[1152]{0:T(1024)}, /*index=5*/f32[1152]{0:T(1024)}, f32[1152]{0:T(1024)}, f32[1152]{0:T(1024)}, f32[1152]{0:T(1024)}) all-reduce(f32[1152]{0:T(1024)S(1)} %dynamic_update_slice.24, ...), channel_id=1, replica_groups=mesh['dp'=16,'tensor'=8] {'dp','tensor'}, use_global_device_ids=true, to_apply=%region_27.28 | all-reduce | flops 13520 | bytes 108160 | tf_op jit(solution)/shard_map/psum | solution.py:278
  (302 shorter events, 225.7 us)
Async XLA Ops:
  8.0 91.6 %all-gather.7.cloned.1.call-start = ((), (), s32[]{:S(2)}) async-start(), calls=%async_computation.10 | async-start | bytes 5308416 | tf_op jit(solution)/shard_map/all_gather | solution.py:101
  14.3 276.2 %reduce-scatter.19.cloned.1.call-start = ((), (), s32[]{:S(2)}) async-start(), calls=%async_computation.11 | async-start | bytes 10616832 | tf_op jit(solution)/shard_map/reduce_scatter | solution.py:141
  166.0 130.3 %all-gather.11.cloned.1.call-start = ((), (), s32[]{:S(2)}) async-start(), calls=%async_computation.13 | async-start | bytes 1566720 | tf_op jit(solution)/shard_map/all_gather | solution.py:95
  166.5 201.1 %all-gather.9.cloned.1.call-start = ((), (), s32[]{:S(2)}) async-start(), calls=%async_computation.12 | async-start | bytes 5308416 | tf_op jit(solution)/shard_map/all_gather | solution.py:151
  294.1 107.0 %all-gather.13.cloned.1.call-start = ((), (), s32[]{:S(2)}) async-start(), calls=%async_computation.14 | async-start | bytes 1566720 | tf_op jit(solution)/shard_map/all_gather | solution.py:97
  294.7 183.6 %all-gather.15.cloned.1.call-start = ((), (), s32[]{:S(2)}) async-start(), calls=%async_computation.16 | async-start | bytes 5308416 | tf_op jit(solution)/shard_map/all_gather | solution.py:177
  295.4 322.2 %reduce-scatter.23.cloned.1.call-start = ((), (), s32[]{:S(2)}) async-start(), calls=%async_computation.17 | async-start | bytes 10616832 | tf_op jit(solution)/shard_map/reduce_scatter | solution.py:184
  495.9 210.9 %reduce-scatter.21.cloned.1.call-start = ((), (), s32[]{:S(2)}) async-start(), calls=%async_computation.15 | async-start | bytes 5308416 | tf_op jit(solution)/shard_map/reduce_scatter | solution.py:155
  506.2 285.4 %all-gather.17.cloned.1.call-start = ((), (), s32[]{:S(2)}) async-start(), calls=%async_computation.18 | async-start | bytes 5308416 | tf_op jit(solution)/shard_map/all_gather | solution.py:193
  711.1 216.2 %reduce-scatter.37.cloned.1.call-start = ((), (), s32[]{:S(2)}) async-start(), calls=%async_computation.25 | async-start | bytes 1566720
  720.3 208.6 %reduce-scatter.35.cloned.1.call-start = ((), (), s32[]{:S(2)}) async-start(), calls=%async_computation.24 | async-start | bytes 1566720
  729.0 202.3 %reduce-scatter.33.cloned.1.call-start = ((), (), s32[]{:S(2)}) async-start(), calls=%async_computation.23 | async-start | bytes 626688
  807.4 160.5 %reduce-scatter.27.cloned.1.call-start = ((), (), s32[]{:S(2)}) async-start(), calls=%async_computation.20 | async-start | bytes 626688 | tf_op jit(solution)/shard_map/reduce_scatter | solution.py:259
  872.4 157.0 %reduce-scatter.29.cloned.1.call-start = ((), (), s32[]{:S(2)}) async-start(), calls=%async_computation.21 | async-start | bytes 626688 | tf_op jit(solution)/shard_map/reduce_scatter | solution.py:262
  878.5 212.6 %reduce-scatter.31.cloned.1.call-start = ((), (), s32[]{:S(2)}) async-start(), calls=%async_computation.22 | async-start | bytes 626688 | tf_op jit(solution)/shard_map/reduce_scatter | solution.py:265
  888.6 295.1 %reduce-scatter.25.cloned.1.call-start = ((), (), s32[]{:S(2)}) async-start(), calls=%async_computation.19 | async-start | bytes 5308416 | tf_op jit(solution)/shard_map/reduce_scatter | solution.py:249
  897.9 285.8 %copy-start.1 = (bf16[256,1152]{1,0:T(8,128)(2,1)S(1)}, bf16[256,1152]{1,0:T(8,128)(2,1)}, u32[]{:S(2)}) copy-start(bf16[256,1152]{1,0:T(8,128)(2,1)} %param.22) | copy-start | bytes 1769476
  897.9 285.7 %copy-start.24 = (f32[1152]{0:T(1024)S(1)}, f32[1152]{0:T(1024)}, u32[]{:S(2)}) copy-start(f32[1152]{0:T(1024)} %copy-done.23) | copy-start | bytes 13828
  897.9 285.7 %copy-start.31 = (f32[256]{0:T(256)S(1)}, f32[256]{0:T(256)}, u32[]{:S(2)}) copy-start(f32[256]{0:T(256)} %copy-done.30) | copy-start | bytes 3076
  897.9 287.4 %copy-start.26 = (f32[1152]{0:T(1024)S(1)}, f32[1152]{0:T(1024)}, u32[]{:S(2)}) copy-start(f32[1152]{0:T(1024)} %get-tuple-element.284) | copy-start | bytes 13828
  897.9 287.4 %copy-start.27 = (f32[1152]{0:T(1024)S(1)}, f32[1152]{0:T(1024)}, u32[]{:S(2)}) copy-start(f32[1152]{0:T(1024)} %get-tuple-element.289) | copy-start | bytes 13828
  897.9 287.4 %copy-start.28 = (f32[1152]{0:T(1024)S(1)}, f32[1152]{0:T(1024)}, u32[]{:S(2)}) copy-start(f32[1152]{0:T(1024)} %get-tuple-element.345) | copy-start | bytes 13828
  898.0 287.4 %copy-start.29 = (f32[1152]{0:T(1024)S(1)}, f32[1152]{0:T(1024)}, u32[]{:S(2)}) copy-start(f32[1152]{0:T(1024)} %get-tuple-element.365) | copy-start | bytes 13828
  898.0 355.6 %copy-start.11 = (f32[256,1152]{1,0:T(8,128)S(1)}, f32[256,1152]{1,0:T(8,128)}, u32[]{:S(2)}) copy-start(f32[256,1152]{1,0:T(8,128)} %get-tuple-element.347) | copy-start | bytes 3538948
  (48 other events, 1557.0 us)
Sparse Core Ops, SparseCore 0:
  14.4 85.1 all-gather.6
  166.1 124.3 reduce-scatter.18
  711.3 80.2 all-gather.16
Sparse Core Ops, SparseCore 1:
  168.2 50.4 all-gather.10
  294.2 73.4 all-gather.8
  369.2 31.8 all-gather.12
  403.4 74.8 all-gather.14
  495.9 121.6 reduce-scatter.22
  621.5 85.1 reduce-scatter.20
  720.4 59.5 reduce-scatter.36
  782.3 62.1 reduce-scatter.34
  846.7 59.3 reduce-scatter.32
  908.6 59.2 reduce-scatter.26
  970.1 59.2 reduce-scatter.28
  1031.9 59.1 reduce-scatter.30
  1094.8 88.7 reduce-scatter.24
where the time goes:
time: 1280 us; the launch traced here: 1260 us
  waiting for transfers between devices  806 us (63%)
  blocking collectives  174 us (14%)
  matrix products  160 us (12%)
  other arithmetic  75.8 us (6%)
  local copies, waits for them, and re-layouts  28.2 us (2%)
  between operations  16.7 us (1%)
    reduce_scatter x1, waiting for transfers between devices, per_device(): lax.psum_scatter(jnp.dot(mixed, out_full, preferred_element_type=jnp.floa...  122 us
    reduce_scatter x1, waiting for transfers between devices, per_device(): lax.psum_scatter(contract_cols(hidden_grad, up_back), 'tensor', scatter_d...  110 us
    reduce_scatter x1, waiting for transfers between devices, per_device(): lax.psum_scatter((part_query + part_key + part_value).astype(jnp.bfloat16...  91.2 us
    reduce_scatter x1, waiting for transfers between devices, per_device(): lax.psum_scatter(jnp.dot(active, down_full, preferred_element_type=jnp.fl...  86.1 us
    all_gather x1, waiting for transfers between devices, per_device(): grad_rows = lax.all_gather(cotangent, 'tensor', axis=0, tiled=True)  77.2 us
    all_gather x1, waiting for transfers between devices, per_device(): lax.all_gather(normed_two.astype(jnp.bfloat16), 'tensor', axis=0, tiled=T...  71.4 us
    psum x1, blocking collectives, per_device(): lax.psum((padded(query_bias_grad, width, tensor_rank * head_cols), padded...  68.2 us
    all_gather x1, waiting for transfers between devices, per_device(): branch_rows = lax.all_gather(branch_low, 'tensor', axis=0, tiled=True)  62.5 us
  transfers between devices with their start and end apart: 16, of which 12 were waited for; matrix products, arithmetic and copies ran while one was open for 13% of the time, Pallas kernels for 0%

commit v1 on v0

v1 whole, which is shorter than its diff:
```python
import functools

import jax
import jax.numpy as jnp
import numpy as np
from jax import lax
from jax.experimental import pallas as pl
from jax.experimental.pallas import tpu as pltpu
from jax.sharding import PartitionSpec as P

HEAD_DIM = 72
EPSILON = 1e-06
CLIP_LIMIT = 2.0
LOWEST = -1e30
SCALE = HEAD_DIM**-0.5

MESH = pl.DeviceIdType.MESH
LOW = jnp.bfloat16
FULL = jnp.float32

WIDTHS = (256, 128, 256, 256)
STARTS = (0, 256, 384, 640)
UNIT = 896
MAIN = 256
TAIL = 13
HIDDEN = 8 * MAIN + 128
PART_ROWS = 48
ORDERS = (("z", "y", "x"), ("x", "z", "y"), ("y", "x", "z"))
STEPS = (1, 3, 2)


def place():
    d, t = lax.axis_index("dp"), lax.axis_index("tensor")
    return {"x": (d // 2) % 4, "y": (t // 4) * 2 + d // 8, "z": t % 4, "core": d % 2}


def device(at):
    return ((at["y"] % 2) * 8 + at["x"] * 2 + at["core"], (at["y"] // 2) * 4 + at["z"])


def moved(at, axis, step):
    other = dict(at)
    other[axis] = 1 - at["core"] if axis == "core" else (at[axis] + step) % 4
    return other


def greet(partners):
    barrier = pltpu.get_barrier_semaphore()
    for partner in partners:
        pl.semaphore_signal(barrier, inc=1, device_id=device(partner), device_id_type=MESH)
    pl.semaphore_wait(barrier, len(partners))


class Copies:
    def __init__(self, send, receive):
        self.send, self.receive, self.used = send, receive, 0

    def start(self, source, target, partner):
        copy = pltpu.make_async_remote_copy(
            src_ref=source,
            dst_ref=target,
            send_sem=self.send.at[self.used],
            recv_sem=self.receive.at[self.used],
            device_id=device(partner),
            device_id_type=MESH,
        )
        self.used += 1
        copy.start()
        return copy


def rects(ref, width, part, have, at):
    xs = slice(None) if "x" in have else at["x"]
    if "y" in have:
        ys = slice(None)
        if "z" in have:
            lanes = [pl.ds(0, 8 * width)]
        else:
            lanes = [pl.ds(pl.multiple_of((h * 4 + at["z"]) * width, 128), width) for h in (0, 1)]
    else:
        ys = at["y"] % 2
        if "z" in have:
            lanes = [pl.ds(pl.multiple_of((at["y"] // 2) * 4 * width, 128), 4 * width)]
        else:
            lanes = [pl.ds(pl.multiple_of(((at["y"] // 2) * 4 + at["z"]) * width, 128), width)]
    return [ref.at[ys, xs, part, :, lane] for lane in lanes]


def gather_kernel(pack, n1, cot, ids, *rest):
    grids, (n1_other, cot_other, ids_other) = rest[:4], rest[4:7]
    both, unit, send, receive, local = rest[7:]
    at = place()
    core = at["core"]
    sibling = moved(at, "core", 1)
    greet([sibling] + [moved(at, axis, step) for axis in "xyz" for step in STEPS])
    copies = Copies(send, receive)
    rows = pl.ds(pl.multiple_of(core * 72, 8), 72)
    first = copies.start(pack.at[1 - core], both.at[rows], sibling)
    others = [
        copies.start(ids, ids_other, sibling),
        copies.start(n1, n1_other, sibling),
        copies.start(cot, cot_other, sibling),
    ]
    both[rows, :] = pack[core]
    first.wait_recv()
    for part in range(3):
        unit[part] = both[part * PART_ROWS : (part + 1) * PART_ROWS, :].astype(LOW)
    count = 0
    held = []
    for part in range(3):
        for grid, width, start in zip(grids, WIDTHS, STARTS):
            (target,) = rects(grid, width, part, (), at)
            copy = pltpu.make_async_copy(
                unit.at[part, :, pl.ds(start, width)], target, local.at[count]
            )
            copy.start()
            held.append(copy)
            count += 1
    for copy in held:
        copy.wait()
    sent = []
    arriving = [[], [], []]
    for phase in range(3):
        for part in range(3):
            for copy in arriving[part]:
                copy.wait_recv()
            have = ORDERS[part][:phase]
            axis = ORDERS[part][phase]
            arriving[part] = []
            for step in STEPS:
                partner = moved(at, axis, step)
                for grid, width in zip(grids, WIDTHS):
                    for view in rects(grid, width, part, have, at):
                        copy = copies.start(view, view, partner)
                        arriving[part].append(copy)
                        sent.append(copy)
    for part in range(3):
        for copy in arriving[part]:
            copy.wait_recv()
    for copy in others:
        copy.wait_recv()
    for copy in [first] + others + sent:
        copy.wait_send()


def hbm():
    return pl.BlockSpec(memory_space=pl.ANY)


def vmem():
    return pl.BlockSpec(memory_space=pltpu.VMEM)


def gather(pack, n1, cot, ids):
    count = 4 + 4 * 3 * 11
    lanes = (2048, 1024, HIDDEN, HIDDEN)
    return pl.pallas_call(
        gather_kernel,
        out_shape=[jax.ShapeDtypeStruct((2, 4, 3, PART_ROWS, lane), LOW) for lane in lanes]
        + [
            jax.ShapeDtypeStruct(n1.shape, LOW),
            jax.ShapeDtypeStruct(cot.shape, LOW),
            jax.ShapeDtypeStruct(ids.shape, FULL),
        ],
        in_specs=[vmem(), hbm(), hbm(), hbm()],
        out_specs=[hbm()] * 7,
        scratch_shapes=[
            pltpu.VMEM((144, UNIT), FULL),
            pltpu.VMEM((3, PART_ROWS, UNIT), LOW),
            pltpu.SemaphoreType.DMA((count,)),
            pltpu.SemaphoreType.DMA((count,)),
            pltpu.SemaphoreType.DMA((12,)),
        ],
        compiler_params=pltpu.CompilerParams(
            collective_id=0, has_side_effects=True, vmem_limit_bytes=16 << 20
        ),
        name="gather_weights",
    )(pack, n1, cot, ids)


def add_up(target, terms, shape):
    lead = int(np.prod(shape[:-2]))

    def index(number, ref):
        where, left = [], number
        for size in reversed(shape[:-2]):
            where.append(left % size)
            left = left // size
        return tuple(reversed(where))

    @pl.loop(0, lead * 3)
    def _(number):
        rows = pl.ds(pl.multiple_of((number % 3) * 16, 16), 16)
        spot = index(number // 3, target) + (rows, slice(None))
        total = terms[0][spot].astype(FULL)
        for term in terms[1:]:
            total = total + term[spot].astype(FULL)
        target[spot] = total.astype(target.dtype)


def first_shape(part, width):
    return ((2, 48, 8 * width), (4, 48, 4 * width), (2, 2, 4, 48, width))[part]


def second_shape(part, width):
    return ((48, 4 * width), (4, 48, width), (2, 2, 48, width))[part]


def first_views(ref, part, at):
    return [ref.at[h] for h in (0, 1)] if part == 2 else [ref]


def second_view(ref, part, width, at):
    if part == 0:
        lanes = pl.ds(pl.multiple_of((at["y"] // 2) * 4 * width, 128), 4 * width)
        return ref.at[at["y"] % 2, :, lanes]
    if part == 1:
        return ref.at[:, :, pl.ds(pl.multiple_of(at["z"] * width, 128), width)]
    return ref.at[:, :, at["x"]]


def third_view(ref, part, width, at):
    if part == 0:
        return ref.at[:, pl.ds(pl.multiple_of(at["z"] * width, 128), width)]
    if part == 1:
        return ref.at[at["x"]]
    return ref.at[at["y"] // 2, at["y"] % 2]


def scatter_kernel(*refs):
    grids, (vector, out, totals) = refs[:4], refs[4:7]
    rest = list(refs[7:])

    def take(count):
        taken, rest[:] = rest[:count], rest[count:]
        return taken

    own1 = [take(4) for _ in range(3)]
    got1 = [take(4) for _ in range(3)]
    sum1 = [take(4) for _ in range(3)]
    got2 = [take(4) for _ in range(3)]
    sum2 = [take(4) for _ in range(3)]
    got3 = [take(4) for _ in range(3)]
    whole, other, line, lines, send, receive, local = rest
    at = place()
    core = at["core"]
    sibling = moved(at, "core", 1)
    greet([sibling] + [moved(at, axis, step) for axis in "xyz" for step in STEPS])
    copies = Copies(send, receive)
    sent = []

    def send_line(phase):
        started = [
            copies.start(line.at[phase], lines.at[phase, k], moved(at, "xyz"[phase], step))
            for k, step in enumerate(STEPS)
        ]
        sent.extend(started)
        return started

    def add_line(phase, started):
        for copy in started:
            copy.wait_recv()
        parts = [line[phase]] + [lines[phase, k] for k in range(3)]
        line[phase + 1, 0:88, :] = (parts[0][:88] + parts[1][:88]) + (parts[2][:88] + parts[3][:88])
        line[phase + 1, 88:96, :] = jnp.maximum(
            jnp.maximum(parts[0][88:], parts[1][88:]), jnp.maximum(parts[2][88:], parts[3][88:])
        )

    line[0] = vector[...]
    lines_out = send_line(0)
    arriving = [[], [], []]
    held = [[], [], []]
    count = 0
    for part in range(3):
        axis, have = ORDERS[part][2], ORDERS[part][:2]
        for k, step in enumerate(STEPS):
            partner = moved(at, axis, step)
            for a in range(4):
                views = rects(grids[a], WIDTHS[a], part, have, partner)
                targets = first_views(got1[part][a].at[k], part, at)
                for view, target in zip(views, targets):
                    copy = copies.start(view, target, partner)
                    arriving[part].append(copy)
                    sent.append(copy)
        for a in range(4):
            views = rects(grids[a], WIDTHS[a], part, have, at)
            for view, target in zip(views, first_views(own1[part][a], part, at)):
                copy = pltpu.make_async_copy(view, target, local.at[count])
                copy.start()
                held[part].append(copy)
                count += 1
    add_line(0, lines_out)
    lines_out = send_line(1)
    arriving2 = [[], [], []]
    for part in range(3):
        for copy in held[part]:
            copy.wait()
        for copy in arriving[part]:
            copy.wait_recv()
        for a in range(4):
            got = got1[part][a]
            add_up(
                sum1[part][a],
                [own1[part][a]] + [got.at[k] for k in range(3)],
                first_shape(part, WIDTHS[a]),
            )
        axis = ORDERS[part][1]
        for k, step in enumerate(STEPS):
            partner = moved(at, axis, step)
            for a in range(4):
                view = second_view(sum1[part][a], part, WIDTHS[a], partner)
                copy = copies.start(view, got2[part][a].at[k], partner)
                arriving2[part].append(copy)
                sent.append(copy)
    add_line(1, lines_out)
    lines_out = send_line(2)
    arriving3 = [[], [], []]
    for part in range(3):
        for copy in arriving2[part]:
            copy.wait_recv()
        for a in range(4):
            got = got2[part][a]
            add_up(
                sum2[part][a],
                [second_view(sum1[part][a], part, WIDTHS[a], at)] + [got.at[k] for k in range(3)],
                second_shape(part, WIDTHS[a]),
            )
        axis = ORDERS[part][0]
        for k, step in enumerate(STEPS):
            partner = moved(at, axis, step)
            for a in range(4):
                view = third_view(sum2[part][a], part, WIDTHS[a], partner)
                copy = copies.start(view, got3[part][a].at[k], partner)
                arriving3[part].append(copy)
                sent.append(copy)
    add_line(2, lines_out)
    last = copies.start(line.at[3], totals.at[core], sibling)
    sent.append(last)
    for part in range(3):
        for copy in arriving3[part]:
            copy.wait_recv()
        for a in range(4):
            got = got3[part][a]
            total = third_view(sum2[part][a], part, WIDTHS[a], at)[...].astype(FULL)
            for k in range(3):
                total = total + got[k].astype(FULL)
            whole[
                part * PART_ROWS : (part + 1) * PART_ROWS, STARTS[a] : STARTS[a] + WIDTHS[a]
            ] = total
    swap = copies.start(
        whole.at[pl.ds(pl.multiple_of((1 - core) * 72, 8), 72)], other, sibling
    )
    sent.append(swap)
    totals[core] = line[3]
    out[core] = whole[pl.ds(pl.multiple_of(core * 72, 8), 72), :]
    swap.wait_recv()
    out[1 - core] = other[...]
    last.wait_recv()
    for copy in sent:
        copy.wait_send()


def scatter(grids, vector):
    count = 3 * 3 + 3 * 4 * (4 + 3 + 3) + 2
    shapes = []
    for part in range(3):
        shapes += [pltpu.VMEM(first_shape(part, w), LOW) for w in WIDTHS]
    for part in range(3):
        shapes += [pltpu.VMEM((3,) + first_shape(part, w), LOW) for w in WIDTHS]
    for part in range(3):
        shapes += [pltpu.VMEM(first_shape(part, w), LOW) for w in WIDTHS]
    for part in range(3):
        shapes += [pltpu.VMEM((3,) + second_shape(part, w), LOW) for w in WIDTHS]
    for part in range(3):
        shapes += [pltpu.VMEM(second_shape(part, w), LOW) for w in WIDTHS]
    for part in range(3):
        shapes += [pltpu.VMEM((3, 48, w), LOW) for w in WIDTHS]
    return pl.pallas_call(
        scatter_kernel,
        out_shape=[
            jax.ShapeDtypeStruct((2, 72, UNIT), FULL),
            jax.ShapeDtypeStruct((2, 96, 128), FULL),
        ],
        in_specs=[hbm()] * 4 + [vmem()],
        out_specs=[vmem()] * 2,
        scratch_shapes=shapes
        + [
            pltpu.VMEM((144, UNIT), FULL),
            pltpu.VMEM((72, UNIT), FULL),
            pltpu.VMEM((4, 96, 128), FULL),
            pltpu.VMEM((3, 3, 96, 128), FULL),
            pltpu.SemaphoreType.DMA((count,)),
            pltpu.SemaphoreType.DMA((count,)),
            pltpu.SemaphoreType.DMA((16,)),
        ],
        compiler_params=pltpu.CompilerParams(
            collective_id=1, has_side_effects=True, vmem_limit_bytes=48 << 20
        ),
        name="scatter_grads",
    )(*grids, vector)


def swap_kernel(mine, theirs, send, receive):
    sibling = moved(place(), "core", 1)
    greet([sibling])
    Copies(send, receive).start(mine, theirs, sibling).wait()


def swap(mine, number):
    return pl.pallas_call(
        swap_kernel,
        out_shape=jax.ShapeDtypeStruct(mine.shape, mine.dtype),
        in_specs=[hbm()],
        out_specs=hbm(),
        scratch_shapes=[pltpu.SemaphoreType.DMA((1,)), pltpu.SemaphoreType.DMA((1,))],
        compiler_params=pltpu.CompilerParams(collective_id=number, has_side_effects=True),
        name=f"swap_{number}",
    )(mine)


def picker(which):
    row = lax.broadcasted_iota(jnp.int32, (256, 128), 0)
    lane = lax.broadcasted_iota(jnp.int32, (256, 128), 1)
    return jnp.where((row == lane + HEAD_DIM * which) & (lane < HEAD_DIM), 1.0, 0.0).astype(LOW)


def placer(which):
    row = lax.broadcasted_iota(jnp.int32, (128, 256), 0)
    lane = lax.broadcasted_iota(jnp.int32, (128, 256), 1)
    return jnp.where((lane == row + HEAD_DIM * which) & (row < HEAD_DIM), 1.0, 0.0).astype(LOW)


def dot(left, right):
    return jnp.dot(left, right, preferred_element_type=FULL)


def dot_rows(left, right):
    return lax.dot_general(left, right, (((0,), (0,)), ((), ())), preferred_element_type=FULL)


def dot_cols(left, right):
    return lax.dot_general(left, right, (((1,), (1,)), ((), ())), preferred_element_type=FULL)


def attend_kernel(
    proj, ids_row, ids_col, mixed, qkv, logsum, peak, q_s, k_s, v_s, out_s, top_s, send, receive, local
):
    at = place()
    z = at["z"]
    partners = [moved(at, "z", step) for step in STEPS]
    greet(partners)
    copies = Copies(send, receive)

    def lanes(index, width):
        return pl.ds(pl.multiple_of(index * width, 128), width)

    started = [
        copies.start(proj.at[:, lanes(partner["z"], 512)], qkv.at[z], partner)
        for partner in partners
    ]
    own = pltpu.make_async_copy(proj.at[:, lanes(z, 512)], qkv.at[z], local.at[0])
    own.start()
    own.wait()
    for copy in started:
        copy.wait_recv()
    for r in range(2):
        for j in range(2):
            for b in range(4):
                block = qkv[b, r * 256 : (r + 1) * 256, j * 256 : (j + 1) * 256]
                spot = slice(b * 256, (b + 1) * 256)
                q_s[2 * r + j, spot, :] = dot(block, picker(0)).astype(LOW)
                k_s[2 * r + j, spot, :] = dot(block, picker(1)).astype(LOW)
                v_s[2 * r + j, spot, :] = dot(block, picker(2)).astype(LOW)
    top_s[...] = jnp.full(top_s.shape, LOWEST, FULL)
    back = []
    for step in STEPS + (0,):
        b = (z + step) % 4
        rows = pl.ds(pl.multiple_of(b * 256, 256), 256)

        @pl.loop(0, 4)
        def _(n, b=b, rows=rows):
            r, j = n // 2, n % 2
            scores = dot_cols(q_s[n, rows, :], k_s[n]) * SCALE
            mine = ids_col[r, rows, :]
            scores = jnp.where(mine == ids_row[r], scores, LOWEST)
            top = jnp.max(scores, axis=1, keepdims=True)
            expo = jnp.exp(scores - top)
            total = jnp.sum(expo, axis=1, keepdims=True)
            weights = (expo * (1.0 / total)).astype(LOW)
            out_s[n, b] = dot(weights, v_s[n]).astype(LOW)
            logsum[n, rows, :] = top + jnp.log(total)
            top_s[n] = jnp.maximum(top_s[n], jnp.where(mine >= 0.0, top, LOWEST))

        for n in range(4):
            r, j = n // 2, n % 2
            source = out_s.at[n, b]
            spot = (pl.ds(r * 256, 256), pl.ds(pl.multiple_of(z * 256 + j * 128, 128), 128))
            if step:
                back.append(copies.start(source, mixed.at[spot], moved(at, "z", step)))
            else:
                copy = pltpu.make_async_copy(source, mixed.at[spot], local.at[1 + n])
                copy.start()
                back.append(copy)
    row = lax.broadcasted_iota(jnp.int32, (8, 128), 0)
    high = [jnp.maximum(jnp.max(top_s[j]), jnp.max(top_s[2 + j])) for j in range(2)]
    peak[...] = jnp.where(row == 0, high[0], high[1])
    for copy in back[:12]:
        copy.wait_recv()
    for copy in back[12:]:
        copy.wait()
    for copy in started + back[:12]:
        copy.wait_send()


def attend(proj, ids_row, ids_col):
    return pl.pallas_call(
        attend_kernel,
        out_shape=[
            jax.ShapeDtypeStruct((512, 1024), LOW),
            jax.ShapeDtypeStruct((4, 512, 512), LOW),
            jax.ShapeDtypeStruct((4, 1024, 1), FULL),
            jax.ShapeDtypeStruct((8, 128), FULL),
        ],
        in_specs=[hbm(), vmem(), vmem()],
        out_specs=[hbm(), vmem(), vmem(), vmem()],
        scratch_shapes=[pltpu.VMEM((4, 1024, 128), LOW)] * 3
        + [
            pltpu.VMEM((4, 4, 256, 128), LOW),
            pltpu.VMEM((4, 256, 1), FULL),
            pltpu.SemaphoreType.DMA((15,)),
            pltpu.SemaphoreType.DMA((15,)),
            pltpu.SemaphoreType.DMA((5,)),
        ],
        compiler_params=pltpu.CompilerParams(
            collective_id=2, has_side_effects=True, vmem_limit_bytes=40 << 20
        ),
        name="attend",
    )(proj, ids_row, ids_col)


def attend_back_kernel(
    upstream, qkv, ids_row, ids_col, logsum, back, grad, q_s, k_s, v_s, g_s, dq_s, dk_s, dv_s, out_s,
    send, receive, local,
):
    at = place()
    z = at["z"]
    partners = [moved(at, "z", step) for step in STEPS]
    greet(partners)
    copies = Copies(send, receive)

    def lanes(index, width):
        return pl.ds(pl.multiple_of(index * width, 128), width)

    started = [
        copies.start(upstream.at[:, lanes(partner["z"], 256)], grad.at[z], partner)
        for partner in partners
    ]
    own = pltpu.make_async_copy(upstream.at[:, lanes(z, 256)], grad.at[z], local.at[0])
    own.start()
    for r in range(2):
        for j in range(2):
            for b in range(4):
                block = qkv[b, r * 256 : (r + 1) * 256, j * 256 : (j + 1) * 256]
                spot = slice(b * 256, (b + 1) * 256)
                q_s[2 * r + j, spot, :] = dot(block, picker(0)).astype(LOW)
                k_s[2 * r + j, spot, :] = dot(block, picker(1)).astype(LOW)
                v_s[2 * r + j, spot, :] = dot(block, picker(2)).astype(LOW)
    own.wait()
    for copy in started:
        copy.wait_recv()
    lane = lax.broadcasted_iota(jnp.int32, (256, 128), 1)
    for r in range(2):
        for j in range(2):
            for b in range(4):
                block = grad[b, r * 256 : (r + 1) * 256, j * 128 : (j + 1) * 128]
                g_s[2 * r + j, b * 256 : (b + 1) * 256, :] = jnp.where(
                    lane < HEAD_DIM, block.astype(FULL), 0.0
                ).astype(LOW)
    sent = []
    for r in range(2):
        for j in range(2):
            n = 2 * r + j
            dk_s[...] = jnp.zeros(dk_s.shape, FULL)
            dv_s[...] = jnp.zeros(dv_s.shape, FULL)

            @pl.loop(0, 4)
            def _(b, n=n, r=r):
                rows = pl.ds(pl.multiple_of(b * 256, 256), 256)
                query, upper = q_s[n, rows, :], g_s[n, rows, :]
                scores = dot_cols(query, k_s[n]) * SCALE
                allowed = ids_col[r, rows, :] == ids_row[r]
                probs = jnp.where(allowed, jnp.exp(scores - logsum[n, rows, :]), 0.0)
                dv_s[...] += dot_rows(probs.astype(LOW), upper)
                prob_grad = dot_cols(upper, v_s[n])
                centre = jnp.sum(probs * prob_grad, axis=1, keepdims=True)
                score_grad = (probs * (prob_grad - centre)).astype(LOW)
                dq_s[rows, :] = (dot(score_grad, k_s[n]) * SCALE).astype(LOW)
                dk_s[...] += dot_rows(score_grad, query)

            for b in range(4):
                spot = slice(b * 256, (b + 1) * 256)
                out_s[b, r * 256 : (r + 1) * 256, j * 256 : (j + 1) * 256] = (
                    dot(dq_s[spot, :], placer(0))
                    + dot((dk_s[spot, :] * SCALE).astype(LOW), placer(1))
                    + dot(dv_s[spot, :].astype(LOW), placer(2))
                ).astype(LOW)
        rows = pl.ds(r * 256, 256)
        for partner in partners:
            source = out_s.at[partner["z"], rows]
            sent.append(copies.start(source, back.at[rows, lanes(z, 512)], partner))
        copy = pltpu.make_async_copy(
            out_s.at[z, rows], back.at[rows, lanes(z, 512)], local.at[1 + r]
        )
        copy.start()
        sent.append(copy)
    for k, copy in enumerate(sent):
        copy.wait()
    for copy in started:
        copy.wait_send()


def attend_back(upstream, qkv, ids_row, ids_col, logsum):
    return pl.pallas_call(
        attend_back_kernel,
        out_shape=jax.ShapeDtypeStruct((512, 2048), LOW),
        in_specs=[hbm(), vmem(), vmem(), vmem(), vmem()],
        out_specs=hbm(),
        scratch_shapes=[pltpu.VMEM((4, 512, 256), LOW)]
        + [pltpu.VMEM((4, 1024, 128), LOW)] * 4
        + [
            pltpu.VMEM((1024, 128), LOW),
            pltpu.VMEM((1024, 128), FULL),
            pltpu.VMEM((1024, 128), FULL),
            pltpu.VMEM((4, 512, 512), LOW),
            pltpu.SemaphoreType.DMA((9,)),
            pltpu.SemaphoreType.DMA((9,)),
            pltpu.SemaphoreType.DMA((3,)),
        ],
        compiler_params=pltpu.CompilerParams(
            collective_id=3, has_side_effects=True, vmem_limit_bytes=40 << 20
        ),
        name="attend_back",
    )(upstream, qkv, ids_row, ids_col, logsum)


def normalize(values, gain, shift):
    centre = values - jnp.mean(values, axis=-1, keepdims=True)
    inverse = lax.rsqrt(jnp.mean(centre * centre, axis=-1, keepdims=True) + EPSILON)
    scaled = centre * inverse
    return (scaled * gain + shift, scaled, inverse)


def normalize_back(upstream, scaled, inverse, gain):
    along = upstream * gain
    width_mean = jnp.mean(along, axis=-1, keepdims=True)
    cross_mean = jnp.mean(along * scaled, axis=-1, keepdims=True)
    return inverse * (along - width_mean - scaled * cross_mean)


def smooth(inner):
    return jax.nn.gelu(inner, approximate=True)


def selector(offset):
    matrix = np.zeros((1024, 128), np.float32)
    for t in range(8):
        for i in range(TAIL):
            matrix[128 * t + offset + i, TAIL * t + i] = 1.0
    return jnp.asarray(matrix, LOW)


def per_device(
    tokens,
    picture,
    cotangent,
    gain_one,
    shift_one,
    query_weight,
    query_bias,
    key_weight,
    value_weight,
    value_bias,
    out_weight,
    out_bias,
    gain_two,
    shift_two,
    up_weight,
    up_bias,
    down_weight,
    down_bias,
):
    width = tokens.shape[1]
    t = lax.axis_index("tensor")
    core = lax.axis_index("dp") % 2
    z = t % 4
    gain_first = gain_one.astype(FULL)
    gain_second = gain_two.astype(FULL)

    out_t = out_weight.astype(FULL).T
    down_t = down_weight.astype(FULL).T
    up = up_weight.astype(FULL)
    halves = []
    for h in range(2):
        cols = slice(h * 72, (h + 1) * 72)
        first = h * (MAIN + TAIL)
        main, tail = slice(first, first + MAIN), slice(first + MAIN, first + MAIN + TAIL)
        halves.append(
            jnp.concatenate(
                [
                    query_weight[:, cols].astype(FULL),
                    key_weight[:, cols].astype(FULL),
                    value_weight[:, cols].astype(FULL),
                    jnp.zeros((72, 40), FULL),
                    out_t[:, cols],
                    up[:, tail],
                    down_t[:, tail],
                    jnp.zeros((72, 30), FULL),
                    up[:, main],
                    down_t[:, main],
                ],
                axis=1,
            )
        )
    pack = jnp.stack(halves)

    inputs = tokens.astype(FULL)
    normed, scaled_one, inverse_one = normalize(inputs, gain_first, shift_one.astype(FULL))
    normed_mine = normed.astype(LOW)
    half = lax.dynamic_slice_in_dim(picture, (t // 4) * 1024, 1024)
    ids = jnp.where(half >= 0, half, -1 - jnp.arange(1024, dtype=jnp.int32)).astype(FULL)
    gq, go, gu, gd, normed_other, cot_other, ids_other = gather(
        pack, normed_mine, cotangent, ids.reshape(8, 128)
    )
    gq, go = gq.reshape(width, 2048), go.reshape(width, 1024)
    select_up, select_down = selector(72), selector(72 + TAIL)
    gu = lax.dynamic_update_slice(
        gu.reshape(width, HIDDEN), dot(go, select_up).astype(LOW), (0, 2048)
    )
    gd = lax.dynamic_update_slice(
        gd.reshape(width, HIDDEN), dot(go, select_down).astype(LOW), (0, 2048)
    )
    both_ids = jnp.stack([ids, ids_other.reshape(1024)])
    ids_row, ids_col = both_ids.reshape(2, 1, 1024), both_ids.reshape(2, 1024, 1)

    def halves_of(vector, size):
        return lax.dynamic_index_in_dim(
            vector.astype(FULL).reshape(8, 2, size), core, axis=1, keepdims=False
        )

    query_b, value_b = halves_of(query_bias, 72), halves_of(value_bias, 72)
    proj_bias = jnp.concatenate(
        [query_b, jnp.zeros((8, 72), FULL), value_b, jnp.zeros((8, 40), FULL)], axis=1
    ).reshape(2048)
    up_b = halves_of(up_bias, MAIN + TAIL)
    hidden_bias = jnp.concatenate(
        [up_b[:, :MAIN].reshape(2048), up_b[:, MAIN:].reshape(8 * TAIL), jnp.zeros((24,), FULL)]
    )

    rows_one = jnp.concatenate([normed_mine, normed_other])
    proj = (dot(rows_one, gq) + proj_bias).astype(LOW)
    mixed, qkv, logsum, peak = attend(proj, ids_row, ids_col)
    part = dot_cols(mixed, go)
    branch = part[:256] + swap(part[256:].astype(LOW), 4).astype(FULL) + out_bias.astype(FULL)
    middle = inputs + branch
    normed_two, scaled_two, inverse_two = normalize(middle, gain_second, shift_two.astype(FULL))
    normed_two = normed_two.astype(LOW)
    rows_two = jnp.concatenate([normed_two, swap(normed_two, 5)])
    hidden = dot(rows_two, gu) + hidden_bias
    active = smooth(hidden).astype(LOW)
    part = dot_cols(active, gd)
    result = middle + (
        part[:256] + swap(part[256:].astype(LOW), 6).astype(FULL) + down_bias.astype(FULL)
    )

    upstream = cotangent.astype(FULL)
    cot_rows = jnp.concatenate([cotangent, cot_other])
    active_grad = dot(cot_rows, gd)
    _, gelu_back = jax.vjp(smooth, hidden)
    hidden_grad = gelu_back(active_grad)[0].astype(LOW)
    part = dot_cols(hidden_grad, gu)
    normed_two_grad = part[:256] + swap(part[256:].astype(LOW), 7).astype(FULL)
    middle_grad = upstream + normalize_back(normed_two_grad, scaled_two, inverse_two, gain_second)
    branch_low = middle_grad.astype(LOW)
    branch_rows = jnp.concatenate([branch_low, swap(branch_low, 8)])
    mixed_grad = dot(branch_rows, go).astype(LOW)
    proj_grad = attend_back(mixed_grad, qkv, ids_row, ids_col, logsum)
    part = dot_cols(proj_grad, gq)
    normed_one_grad = part[:256] + swap(part[256:].astype(LOW), 9).astype(FULL)
    input_grad = middle_grad + normalize_back(normed_one_grad, scaled_one, inverse_one, gain_first)

    grad_q = dot_rows(rows_one, proj_grad).astype(LOW)
    grad_u = dot_rows(rows_two, hidden_grad[:, :2048]).astype(LOW)
    grad_d = dot_rows(cot_rows, active[:, :2048]).astype(LOW)
    up_tail = dot_cols(hidden_grad[:, 2048:], select_up).astype(LOW)
    down_tail = dot_cols(active[:, 2048:], select_down).astype(LOW)
    grad_o = dot_rows(
        jnp.concatenate([branch_rows, rows_two, cot_rows]),
        jnp.concatenate([mixed, up_tail, down_tail]),
    ).astype(LOW)

    head = lax.broadcasted_iota(jnp.int32, (8, 128), 1)
    peaks = jnp.where(
        head == 4 * z + core,
        peak[0, 0],
        jnp.where(head == 4 * z + 2 + core, peak[1, 0], LOWEST),
    )

    def total(values):
        return jnp.sum(values.astype(FULL), axis=0)

    vector = jnp.concatenate(
        [
            total(proj_grad),
            total(hidden_grad),
            total(branch_low),
            total(upstream),
            total(normed_one_grad * scaled_one),
            total(normed_one_grad),
            total(normed_two_grad * scaled_two),
            total(normed_two_grad),
            jnp.zeros((128,), FULL),
        ]
    ).reshape(88, 128)
    vector = jnp.concatenate([vector, peaks])
    shape = (2, 4, 3, PART_ROWS)
    grads, totals = scatter(
        [
            grad_q.reshape(shape + (2048,)),
            grad_o.reshape(shape + (1024,)),
            grad_u.reshape(shape + (2048,)),
            grad_d.reshape(shape + (2048,)),
        ],
        vector,
    )

    def side(first, size):
        return jnp.concatenate([grads[0, :, first : first + size], grads[1, :, first : first + size]], axis=1)

    def hidden_side(main, tail):
        return jnp.concatenate(
            [
                grads[0, :, main : main + MAIN],
                grads[0, :, tail : tail + TAIL],
                grads[1, :, main : main + MAIN],
                grads[1, :, tail : tail + TAIL],
            ],
            axis=1,
        )

    query_w, key_w, value_w = side(0, 72), side(72, 72), side(144, 72)
    out_w = side(256, 72).T
    up_w = hidden_side(384, 256 + 72)
    down_w = hidden_side(640, 256 + 72 + TAIL).T
    flat = totals[:, :88].reshape(2, 88 * 128)
    heads = flat[:, :2048].reshape(2, 8, 256)
    query_b_grad = heads[:, :, :72].transpose(1, 0, 2).reshape(width)
    value_b_grad = heads[:, :, 144:216].transpose(1, 0, 2).reshape(width)
    up_b_grad = (
        jnp.concatenate(
            [
                flat[:, 2048:4096].reshape(2, 8, MAIN),
                flat[:, 4096 : 4096 + 8 * TAIL].reshape(2, 8, TAIL),
            ],
            axis=2,
        )
        .transpose(1, 0, 2)
        .reshape(-1)
    )
    summed = (flat[0] + flat[1])[2048 + HIDDEN : 2048 + HIDDEN + 6 * width].reshape(6, width)
    high = jnp.maximum(totals[0, 88, :16], totals[1, 88, :16])
    factor = jnp.sqrt(CLIP_LIMIT / jnp.maximum(high, CLIP_LIMIT))
    column_factor = jnp.repeat(lax.dynamic_slice_in_dim(factor, 2 * t, 2), HEAD_DIM)
    clipped_query = query_weight.astype(FULL) * column_factor[None, :]
    clipped_key = key_weight.astype(FULL) * column_factor[None, :]
    return (
        result,
        input_grad,
        query_w,
        key_w,
        value_w,
        out_w,
        up_w,
        down_w,
        query_b_grad,
        value_b_grad,
        up_b_grad,
        summed[0],
        summed[1],
        summed[2],
        summed[3],
        summed[4],
        summed[5],
        clipped_query,
        clipped_key,
    )


def solution(mesh):
    in_specs = (
        P(("dp", "tensor"), None),
        P("dp"),
        P(("dp", "tensor"), None),
        P(),
        P(),
        P("dp", "tensor"),
        P(),
        P("dp", "tensor"),
        P("dp", "tensor"),
        P(),
        P("tensor", "dp"),
        P(),
        P(),
        P(),
        P("dp", "tensor"),
        P(),
        P("tensor", "dp"),
        P(),
    )
    out_specs = (
        P(("dp", "tensor"), None),
        P(("dp", "tensor"), None),
        P("dp", "tensor"),
        P("dp", "tensor"),
        P("dp", "tensor"),
        P("tensor", "dp"),
        P("dp", "tensor"),
        P("tensor", "dp"),
        P(),
        P(),
        P(),
        P(),
        P(),
        P(),
        P(),
        P(),
        P(),
        P("dp", "tensor"),
        P("dp", "tensor"),
    )
    return jax.shard_map(
        per_device, mesh=mesh, in_specs=in_specs, out_specs=out_specs, check_vma=False
    )
```

time: 1280 us -> 461 us (0.36)
  waiting for transfers between devices: 806 us -> 0 us
  Pallas kernels: 0 us -> 317 us
  blocking collectives: 174 us -> 0 us
  matrix products: 160 us -> 72.1 us
  other arithmetic: 75.8 us -> 27.6 us
  between operations: 16.7 us -> 2.03 us
    reduce_scatter x7 -> x0, waiting for transfers between devices: 565 us -> none  [the longest x1 122 us: per_device(): lax.psum_scatter(jnp.dot(mixed, out_full, preferred_element_type=jnp.floa...]
    pallas_call x0 -> x10, Pallas kernels: none -> 317 us  [the longest x1 104 us: scatter(): pl.pallas_call(scatter_kernel, out_shape=[jax.ShapeDtypeStruct((2, 72, UN...]
    all_gather x6 -> x0, waiting for transfers between devices: 239 us -> none  [the longest x1 77.2 us: per_device(): grad_rows = lax.all_gather(cotangent, 'tensor', axis=0, tiled=True)]
    dot_general x46 -> x16, matrix products: 160 us -> 72.1 us  [the longest x6 33.5 us: dot(): return jnp.dot(left, right, preferred_element_type=FULL)]
    all_gather x4 -> x0, blocking collectives: 78.3 us -> none  [the longest x1 22.8 us: per_device(): lax.all_gather(out_weight, 'dp', axis=1, tiled=True)]
    psum x1 -> x0, blocking collectives: 68.2 us -> none  [per_device(): lax.psum((padded(query_bias_grad, width, tensor_rank * head_cols), padded...]
    pmax x1 -> x0, blocking collectives: 27.6 us -> none  [per_device(): global_peak = lax.pmax(jnp.max(peaks, axis=0), 'dp')]
    convert_element_type x22 -> x11, other arithmetic: 28.8 us -> 3.27 us  [the longest x1 1.12 us: per_device(): normed_two = normed_two.astype(LOW)]
  transfers between devices with their start and end apart: 16 -> 0, of which waited for: 12 -> 0; matrix products, arithmetic and copies ran while one was open for 13% -> 0% of each run, Pallas kernels for 0% -> 0%
where the time goes in v1:
time: 461 us; the launch traced here: 453 us
  Pallas kernels  317 us (69%)
  matrix products  72.1 us (16%)
  local copies, waits for them, and re-layouts  34.1 us (7%)
  other arithmetic  27.6 us (6%)
    pallas_call x1, Pallas kernels, scatter(): pl.pallas_call(scatter_kernel, out_shape=[jax.ShapeDtypeStruct((2, 72, UN...  104 us
    pallas_call x1, Pallas kernels, gather(): pl.pallas_call(gather_kernel, out_shape=[jax.ShapeDtypeStruct((2, 4, 3, P...  95.7 us
    pallas_call x1, Pallas kernels, attend_back(): pl.pallas_call(attend_back_kernel, out_shape=jax.ShapeDtypeStruct((512, 2...  54.8 us
    pallas_call x1, Pallas kernels, attend(): pl.pallas_call(attend_kernel, out_shape=[jax.ShapeDtypeStruct((512, 1024)...  44 us
    dot_general x6, matrix products, dot(): return jnp.dot(left, right, preferred_element_type=FULL)  33.5 us
    unnamed x133, local copies, waits for them, and re-layouts  22.2 us
    dot_general x4, matrix products, dot_rows(): lax.dot_general(left, right, (((0,), (0,)), ((), ())), preferred_element_...  19.5 us
    dot_general x6, matrix products, dot_cols(): lax.dot_general(left, right, (((1,), (1,)), ((), ())), preferred_element_...  19 us

profile of v1, /device:TPU:1, one launch (start us, length us, event | category | flops | bytes accessed | tf_op | source)
XLA Modules:
  0.0 452.7 jit_solution(11548106337424534420)
XLA Ops:
  8.1 95.7 %gather_weights.1 = (bf16[2,4,3,48,2048]{4,3,2,1,0:T(8,128)(2,1)S(1)}, bf16[2,4,3,48,1024]{4,3,2,1,0:T(8,128)(2,1)S(1)}, bf16[2,4,3,48,2176]{4,3,2,1,0:T(8,128)(...) custom-call(f32[2,72,896]{2,1,0:T(8,128)S(1)} %pad_maximum_fusion.6., ...), custom_call_target="tpu_custom_call" | custom-call | tf_op jit(solution)/shard_map/gather_weights/pallas_call | solution.py:157
  112.5 6.8 %add_convert_fusion.proj = bf16[512,2048]{1,0:T(8,128)(2,1)} fusion(bf16[1152,2048]{1,0:T(8,128)(2,1)} %bitcast.124, f32[2048]{0:T(1024)S(1)} %bitcast.148, bf16[256,1152]{1,0:T(8,128)(2,1)S(1)} %get-tuple-element.32, bf16[256,1152]{1,0:T(8,128)(2,1)S(1)} %fusion.23.n1), kind=kOutput, calls=%fused_computation.16 | convolution fusion | flops 2420375552 | bytes 8003584 | tf_op jit(solution)/shard_map/dot_general | solution.py:434
  121.3 44.0 %attend.1 = (bf16[512,1024]{1,0:T(8,128)(2,1)S(1)}, bf16[4,512,512]{2,1,0:T(8,128)(2,1)S(1)}, f32[4,1024,1]{2,1,0:T(8,128)S(1)}, f32[8,128]{1,0:T(8,128)S(1)}) custom-call(bf16[512,2048]{1,0:T(8,128)(2,1)S(1)} %copy-done.7, f32[2,1,1024]{2,1,0:T(1,128)S(1)} %reshape.205.ids_row, f32[2,1024,1]{2,1,0:T(8,128)S(1)} %copy.48.ids_col), custom_call_target="tpu_custom_call" | custom-call | tf_op jit(solution)/shard_map/attend/pallas_call | solution.py:516
  169.9 4.8 %swap_4.1 = bf16[256,1152]{1,0:T(8,128)(2,1)} custom-call(bf16[256,1152]{1,0:T(8,128)(2,1)} %slice.419.mine), custom_call_target="tpu_custom_call" | custom-call | tf_op jit(solution)/shard_map/swap_4/pallas_call | solution.py:410
  178.8 2.4 swap_5.1
  181.2 3.3 fusion.13
  187.2 7.2 %fusion.60 = f32[512,2176]{1,0:T(8,128)} fusion(bf16[512,1152]{1,0:T(8,128)(2,1)S(1)} %constant_dynamic-update-slice_fusion, bf16[1152,2176]{1,0:T(8,128)(2,1)} %fusion.12), kind=kOutput, calls=%fused_computation.182 | convolution fusion | flops 2566914048 | bytes 10649600 | tf_op jit(solution)/shard_map/dot_general | solution.py:434
  194.8 10.9 %convert_reduce_fusion = (f32[2176]{0:T(1024)}, bf16[512,2176]{1,0:T(8,128)(2,1)}, bf16[512,2176]{1,0:T(8,128)(2,1)S(1)}) fusion(f32[512,2176]{1,0:T(8,128)} %fusion.60, f32[2176]{0:T(1024)S(1)} %concatenate.63, bf16[1152,2176]{1,0:T(8,128)(2,1)} %fusion.13, bf16[256,1152]{1,0:T(8,128)(2,1)} %swap_5.1, bf16[256,1152]{1,0:T(8,128)(2,1)} %add_convert_fusion.1.mine), kind=kOutput, calls=%fused_computation.13 | convolution fusion | flops 2597124096 | bytes 15123456 | tf_op jit(solution)/shard_map/dot_general | solution.py:434
  205.7 6.4 %fusion.59 = f32[512,1152]{1,0:T(8,128)S(1)} fusion(bf16[512,2176]{1,0:T(8,128)(2,1)S(1)} %get-tuple-element.117, bf16[1152,2176]{1,0:T(8,128)(2,1)} %fusion.12), kind=kOutput, calls=%fused_computation.181 | convolution fusion | flops 2566914048 | bytes 9601024 | tf_op jit(solution)/shard_map/dot_general | solution.py:442
  214.4 2.4 swap_6.1
  216.8 6.3 %fusion.61 = f32[512,1152]{1,0:T(8,128)S(1)} fusion(bf16[512,2176]{1,0:T(8,128)(2,1)} %get-tuple-element.114, bf16[1152,2176]{1,0:T(8,128)(2,1)} %fusion.13), kind=kOutput, calls=%fused_computation.183 | convolution fusion | flops 2566914048 | bytes 9601024 | tf_op jit(solution)/shard_map/dot_general | solution.py:442
  227.8 2.5 multiply_reduce_fusion
  230.4 4.0 convert_reduce_fusion.4
  236.9 3.7 convolution_convert_fusion.8.upstream
  240.6 54.8 %attend_back.1 = bf16[512,2048]{1,0:T(8,128)(2,1)S(1)} custom-call(bf16[512,1024]{1,0:T(8,128)(2,1)S(1)} %convolution_convert_fusion.8.upstream, bf16[4,512,512]{2,1,0:T(8,128)(2,1)S(1)} %copy-done.4, f32[2,1,1024]{2,1,0:T(1,128)S(1)} %reshape.205.ids_row, f32[2,1024,1]{2,1,0:T(8,128)S(1)} %copy.48.ids_col, f32[4,1024,1]{2,1,0:T(8,128)S(1)} %copy-done.6), custom_call_target="tpu_custom_call" | custom-call | tf_op jit(solution)/shard_map/attend_back/pallas_call | solution.py:623
  295.9 2.9 fusion.62
  301.1 3.8 swap_9.1
  304.9 2.7 fusion.28
  309.6 6.8 %convolution_convert_fusion.1 = bf16[1152,2048]{1,0:T(8,128)(2,1)} fusion(bf16[512,2176]{1,0:T(8,128)(2,1)} %get-tuple-element.114, bf16[256,1152]{1,0:T(8,128)(2,1)} %swap_5.1, bf16[256,1152]{1,0:T(8,128)(2,1)} %add_convert_fusion.1.mine), kind=kOutput, calls=%fused_computation.1 | convolution fusion | flops 2420637696 | bytes 7995392 | tf_op jit(solution)/shard_map/dot_general | solution.py:438
  321.3 4.1 convolution_convert_fusion.3
  325.4 4.3 convolution_convert_fusion
  329.7 4.3 convolution_convert_fusion.2
  334.0 104.3 %scatter_grads.1 = (f32[2,72,896]{2,1,0:T(8,128)S(1)}, f32[2,96,128]{2,1,0:T(8,128)S(1)}) custom-call(bf16[2,4,3,48,2048]{4,3,2,1,0:T(8,128)(2,1)} %bitcast.134, bf16[2,4,3,48,1024]{4,3,2,1,0:T(8,128)(2,1)S(1)} %bitcast.120, bf16[2,4,3,48,2048]{4,3,2,1,0:T(8,128)(2,1)} %bitcast.132, bf16[2,4,3,48,2048]{4,3,2,1,0:T(8,128)(2,1)} %bitcast.133, ...), custom_call_target="tpu_custom_call" | custom-call | tf_op jit(solution)/shard_map/scatter_grads/pallas_call | solution.py:378
  449.7 2.8 fusion.27
  (230 shorter events, 59.3 us)
Async XLA Ops:
  0.7 6.6 %copy-start.19 = (bf16[256,1152]{1,0:T(8,128)(2,1)S(1)}, bf16[256,1152]{1,0:T(8,128)(2,1)}, u32[]{:S(2)}) copy-start(bf16[256,1152]{1,0:T(8,128)(2,1)} %param.20) | copy-start | bytes 1769476
  7.3 104.7 %copy-start.48 = (bf16[1152]{0:T(1024)(128)(2,1)S(1)}, bf16[1152]{0:T(1024)(128)(2,1)}, u32[]{:S(2)}) copy-start(bf16[1152]{0:T(1024)(128)(2,1)} %param.26) | copy-start | bytes 6916
  7.3 104.8 %copy-start.49 = (bf16[1152]{0:T(1024)(128)(2,1)S(1)}, bf16[1152]{0:T(1024)(128)(2,1)}, u32[]{:S(2)}) copy-start(bf16[1152]{0:T(1024)(128)(2,1)} %param.29) | copy-start | bytes 6916
  7.8 297.1 %copy-start.39 = (f32[256]{0:T(256)}, f32[256]{0:T(256)S(1)}, u32[]{:S(2)}) copy-start(f32[256]{0:T(256)S(1)} %add_rsqrt_fusion.1) | copy-start | bytes 3076
  112.4 6.8 %copy-start.43 = (s32[2048]{0:T(1024)S(1)}, s32[2048]{0:T(1024)}, u32[]{:S(2)}) copy-start(s32[2048]{0:T(1024)} %param.21) | copy-start | bytes 24580
  121.3 44.0 %copy-start.12 = (bf16[2,4,3,48,1024]{4,3,2,1,0:T(8,128)(2,1)S(1)}, bf16[2,4,3,48,1024]{4,3,2,1,0:T(8,128)(2,1)}, u32[]{:S(2)}) copy-start(bf16[2,4,3,48,1024]{4,3,2,1,0:T(8,128)(2,1)} %copy-done.11) | copy-start | bytes 7077892
  169.0 5.7 %copy-start.50 = (bf16[1152]{0:T(1024)(128)(2,1)S(1)}, bf16[1152]{0:T(1024)(128)(2,1)}, u32[]{:S(2)}) copy-start(bf16[1152]{0:T(1024)(128)(2,1)} %param.31) | copy-start | bytes 6916
  187.2 7.2 %copy-start.42 = (bf16[4304]{0:T(1024)(128)(2,1)S(1)}, bf16[4304]{0:T(1024)(128)(2,1)}, u32[]{:S(2)}) copy-start(bf16[4304]{0:T(1024)(128)(2,1)} %param.35) | copy-start | bytes 25828
  205.7 6.5 %copy-start.44 = (bf16[512,2176]{1,0:T(8,128)(2,1)}, bf16[512,2176]{1,0:T(8,128)(2,1)S(1)}, u32[]{:S(2)}) copy-start(bf16[512,2176]{1,0:T(8,128)(2,1)S(1)} %get-tuple-element.117) | copy-start | bytes 6684676
  225.4 5.0 %copy-start.53 = (bf16[1152]{0:T(1024)(128)(2,1)S(1)}, bf16[1152]{0:T(1024)(128)(2,1)}, u32[]{:S(2)}) copy-start(bf16[1152]{0:T(1024)(128)(2,1)} %param.37) | copy-start | bytes 6916
  236.8 3.7 copy-start.4
  236.9 59.0 %slice-start = ((s8[4718592]{0:T(1024)(128)(4,1)}), s8[4194304]{0:T(1024)(128)(4,1)S(1)}, s32[]{:S(2)}) async-start(s8[4718592]{0:T(1024)(128)(4,1)} %bitcast.125), calls=%async_computation | async-start | bytes 8388608
  240.6 55.2 %copy-start.41 = (f32[2176]{0:T(1024)S(1)}, f32[2176]{0:T(1024)}, u32[]{:S(2)}) copy-start(f32[2176]{0:T(1024)} %get-tuple-element.113) | copy-start | bytes 26116
  240.6 55.3 %slice-start.1 = ((s8[4718592]{0:T(1024)(128)(4,1)}), s8[524288]{0:T(1024)(128)(4,1)S(1)}, s32[]{:S(2)}) async-start(s8[4718592]{0:T(1024)(128)(4,1)} %bitcast.125), calls=%async_computation.1 | async-start | bytes 1048576
  300.2 4.7 %copy-start.20 = (bf16[256,1152]{1,0:T(8,128)(2,1)S(1)}, bf16[256,1152]{1,0:T(8,128)(2,1)}, u32[]{:S(2)}) copy-start(bf16[256,1152]{1,0:T(8,128)(2,1)} %param.20) | copy-start | bytes 1769476
  309.6 6.9 %copy-start.21 = (bf16[256,1152]{1,0:T(8,128)(2,1)S(1)}, bf16[256,1152]{1,0:T(8,128)(2,1)}, u32[]{:S(2)}) copy-start(bf16[256,1152]{1,0:T(8,128)(2,1)} %get-tuple-element.111.mine) | copy-start | bytes 1769476
  309.6 6.9 %copy-start.29 = (bf16[256,1152]{1,0:T(8,128)(2,1)S(1)}, bf16[256,1152]{1,0:T(8,128)(2,1)}, u32[]{:S(2)}) copy-start(bf16[256,1152]{1,0:T(8,128)(2,1)} %swap_8.1) | copy-start | bytes 1769476
  321.3 4.1 copy-start.33
  325.4 4.3 copy-start.2
  438.3 8.8 %copy-start.37 = (bf16[72,144]{1,0:T(8,128)(2,1)S(1)}, bf16[72,144]{1,0:T(8,128)(2,1)}, u32[]{:S(2)}) copy-start(bf16[72,144]{1,0:T(8,128)(2,1)} %param.25) | copy-start | bytes 62212
  438.4 8.8 %copy-start.38 = (bf16[72,144]{1,0:T(8,128)(2,1)S(1)}, bf16[72,144]{1,0:T(8,128)(2,1)}, u32[]{:S(2)}) copy-start(bf16[72,144]{1,0:T(8,128)(2,1)} %param.27) | copy-start | bytes 62212
  438.4 11.3 %copy-start.23 = (bf16[256,1152]{1,0:T(8,128)(2,1)S(1)}, bf16[256,1152]{1,0:T(8,128)(2,1)}, u32[]{:S(2)}) copy-start(bf16[256,1152]{1,0:T(8,128)(2,1)} %swap_9.1) | copy-start | bytes 1769476
  438.4 11.3 %copy-start.24 = (f32[256,1152]{1,0:T(8,128)S(1)}, f32[256,1152]{1,0:T(8,128)}, u32[]{:S(2)}) copy-start(f32[256,1152]{1,0:T(8,128)} %get-tuple-element.112) | copy-start | bytes 3538948
  438.4 11.3 %copy-start.40 = (f32[256]{0:T(256)S(1)}, f32[256]{0:T(256)}, u32[]{:S(2)}) copy-start(f32[256]{0:T(256)} %copy-done.39) | copy-start | bytes 3076
  (32 other events, 68.6 us)

commit v2 on v1

v2 whole, which is shorter than its diff:
```python
import functools

import jax
import jax.numpy as jnp
import numpy as np
from jax import lax
from jax.experimental import pallas as pl
from jax.experimental.pallas import tpu as pltpu
from jax.sharding import PartitionSpec as P

HEAD_DIM = 72
EPSILON = 1e-06
CLIP_LIMIT = 2.0
LOWEST = -1e30
SCALE = HEAD_DIM**-0.5

MESH = pl.DeviceIdType.MESH
LOW = jnp.bfloat16
FULL = jnp.float32

WIDTHS = (256, 128, 256, 256)
STARTS = (0, 256, 384, 640)
UNIT = 896
MAIN = 256
TAIL = 13
HIDDEN = 8 * MAIN + 128
PARTS = ((0, 48, "zyx"), (48, 48, "xzy"), (96, 48, "yxz"))
PARTS_BEHIND = ((0, 64, "zyx"), (64, 64, "zxy"), (128, 16, "yxz"))
STEPS = (1, 3, 2)
ALL = "xyz"


def place():
    d, t = lax.axis_index("dp"), lax.axis_index("tensor")
    return {"x": (d // 2) % 4, "y": (t // 4) * 2 + d // 8, "z": t % 4, "core": d % 2}


def device(at):
    return ((at["y"] % 2) * 8 + at["x"] * 2 + at["core"], (at["y"] // 2) * 4 + at["z"])


def moved(at, axis, step):
    other = dict(at)
    other[axis] = 1 - at["core"] if axis == "core" else (at[axis] + step) % 4
    return other


def greet(partners):
    barrier = pltpu.get_barrier_semaphore()
    for partner in partners:
        pl.semaphore_signal(barrier, inc=1, device_id=device(partner), device_id_type=MESH)
    pl.semaphore_wait(barrier, len(partners))


class Copies:
    def __init__(self, send, receive):
        self.send, self.receive, self.used = send, receive, 0

    def start(self, source, target, partner):
        copy = pltpu.make_async_remote_copy(
            src_ref=source,
            dst_ref=target,
            send_sem=self.send.at[self.used],
            recv_sem=self.receive.at[self.used],
            device_id=device(partner),
            device_id_type=MESH,
        )
        self.used += 1
        copy.start()
        return copy


def lanes(first, size):
    return pl.ds(first if isinstance(first, int) else pl.multiple_of(first, 128), size)


def spots(held, have, at, width, rows, half=None):
    zs, ys = (4 if "z" in held else 1), at["y"] if "y" in held else 0
    x_at = pl.ds(0, 4) if "x" in have else pl.ds(at["x"] if "x" in held else 0, 1)
    y_at = pl.ds(0, 2) if "y" in have else pl.ds(ys % 2, 1)
    z = at["z"] if "z" in held else 0
    if "y" in have and "z" in have:
        ranges = [(0, 8 * width)]
    elif "y" in have:
        ranges = [((h * zs + z) * width, width) for h in (0, 1)]
    elif "z" in have:
        ranges = [((ys // 2) * zs * width, 4 * width)]
    else:
        ranges = [(((ys // 2) * zs + z) * width, width)]
    if half is not None:
        if len(ranges) == 2:
            ranges = [ranges[half]]
        elif "x" in have:
            x_at = pl.ds(2 * half, 2)
        elif "y" in have:
            y_at = pl.ds(half, 1)
        else:
            ((first, size),) = ranges
            ranges = [(first + half * (size // 2), size // 2)]
    return [(y_at, x_at, pl.ds(*rows), lanes(*r)) for r in ranges]


def rect_shape(have, width, rows):
    ys, xs, zs = 2 if "y" in have else 1, 4 if "x" in have else 1, 4 if "z" in have else 1
    return (ys, xs, rows, ys * zs * width)


class Gather:
    def __init__(self, copies, at, grids, widths, part):
        self.copies, self.at, self.grids, self.widths = copies, at, grids, widths
        self.rows, self.order = part[:2], part[2]
        self.arriving, self.sent = [], []

    def views(self, grid, width, have, at, half=None):
        return [grid.at[spot] for spot in spots(ALL, have, at, width, self.rows, half)]

    def send(self, have, owner, partner, half=None):
        started = []
        for grid, width in zip(self.grids, self.widths):
            for view in self.views(grid, width, have, owner, half):
                started.append(self.copies.start(view, view, partner))
        self.sent += started
        return started

    def settle(self):
        for copy in self.arriving:
            copy.wait_recv()
        self.arriving = []

    def first(self):
        for step in STEPS:
            self.arriving += self.send("", self.at, moved(self.at, self.order[0], step))

    def ring(self, phase):
        self.settle()
        axis, have = self.order[phase], self.order[:phase]
        self.after = self.send(have, self.at, moved(self.at, axis, 1))
        self.before = self.send(have, self.at, moved(self.at, axis, 3))

    def forward(self, phase):
        axis, have = self.order[phase], self.order[:phase]
        up, down = moved(self.at, axis, 1), moved(self.at, axis, 3)
        for copy in self.after:
            copy.wait_recv()
        self.arriving += self.send(have, down, up, 0)
        for copy in self.before:
            copy.wait_recv()
        self.arriving += self.send(have, up, down, 1)


def add_into(target, terms, shape):
    @pl.loop(0, shape[0] * shape[1] * (shape[2] // 16))
    def _(n):
        block = n // (shape[2] // 16)
        spot = (
            block // shape[1],
            block % shape[1],
            pl.ds(pl.multiple_of((n % (shape[2] // 16)) * 16, 16), 16),
            slice(None),
        )
        total = terms[0][spot].astype(FULL)
        for term in terms[1:]:
            total = total + term[spot].astype(FULL)
        target[spot] = total.astype(target.dtype)


def half_shape(have, shape):
    ys, xs, rows, cols = shape
    if "y" in have and "z" not in have:
        return (ys, xs, rows, cols // 2)
    if "x" in have:
        return (ys, 2, rows, cols)
    if "y" in have:
        return (1, xs, rows, cols)
    return (ys, xs, rows, cols // 2)


class Scatter:
    BUFFERS = 5 + 5 + 1

    @staticmethod
    def shapes(widths, part):
        _, rows, order = part
        shapes = []
        for have in (order[:2], order[:1]):
            for _ in range(5):
                shapes += [pltpu.VMEM(rect_shape(have, w, rows), LOW) for w in widths]
        shapes += [pltpu.VMEM((3, 1, 1, rows, w), LOW) for w in widths]
        return shapes

    def __init__(self, copies, at, grids, widths, part, buffers, local):
        self.copies, self.at, self.grids, self.widths = copies, at, grids, widths
        self.rows, self.order = part[:2], part[2]
        n = len(widths)
        groups = [buffers[k * n : (k + 1) * n] for k in range(self.BUFFERS)]
        self.near, self.mix, self.low, self.high, self.own = (
            [groups[0], groups[5]],
            [groups[1], groups[6]],
            [groups[2], groups[7]],
            [groups[3], groups[8]],
            [groups[4], groups[9]],
        )
        self.direct = groups[10]
        self.local = local
        self.sent = []

    def source(self, phase, a, at, half=None):
        have = self.order[: 2 - phase]
        if phase == 0:
            found = spots(ALL, have, at, self.widths[a], self.rows, half)
            return [self.grids[a].at[spot] for spot in found]
        held = self.order[: 3 - phase]
        found = spots(held, have, at, self.widths[a], (0, self.rows[1]), half)
        return [self.own[phase - 1][a].at[spot] for spot in found]

    def target(self, phase, buffer, a, half=None):
        have = self.order[: 2 - phase]
        found = spots(have, have, self.at, self.widths[a], (0, self.rows[1]), half)
        return [buffer[phase][a].at[spot] for spot in found]

    def push(self, sources, targets, partner):
        started = [self.copies.start(s, t, partner) for s, t in zip(sources, targets)]
        self.sent += started
        return started

    def begin(self, phase):
        axis = self.order[2 - phase]
        up, down, far = (moved(self.at, axis, step) for step in STEPS)
        self.arriving, self.loading = [], []
        for a in range(len(self.grids)):
            for half, partner in ((0, up), (1, down)):
                self.arriving += self.push(
                    self.source(phase, a, far, half),
                    self.target(phase, self.near, a, half),
                    partner,
                )
        if phase == 0:
            for a in range(len(self.grids)):
                pairs = list(
                    zip(
                        self.source(0, a, up, 0) + self.source(0, a, down, 1),
                        self.target(0, self.mix, a, 0) + self.target(0, self.mix, a, 1),
                    )
                )
                pairs += list(zip(self.source(0, a, self.at), self.target(0, self.own, a)))
                for view, target in pairs:
                    copy = pltpu.make_async_copy(view, target, self.local[0].at[self.local[1]])
                    self.local[1] += 1
                    copy.start()
                    self.loading.append(copy)

    def relay(self, phase):
        axis = self.order[2 - phase]
        have = self.order[: 2 - phase]
        up, down, _ = (moved(self.at, axis, step) for step in STEPS)
        for copy in self.loading:
            copy.wait()
        for copy in self.arriving:
            copy.wait_recv()
        self.arriving = []
        for a in range(len(self.grids)):
            shape = half_shape(have, rect_shape(have, self.widths[a], self.rows[1]))
            for half, partner in ((0, up), (1, down)):
                (mix,) = self.target(phase, self.mix, a, half)
                (near,) = self.target(phase, self.near, a, half)
                if phase == 0:
                    add_into(mix, [mix, near], shape)
                else:
                    (view,) = self.source(phase, a, partner, half)
                    add_into(mix, [view, near], shape)
                buffer = self.low if half == 0 else self.high
                self.arriving += self.push(
                    [mix] + self.source(phase, a, partner, 1 - half),
                    self.target(phase, buffer, a, half) + self.target(phase, buffer, a, 1 - half),
                    partner,
                )

    def finish(self, phase):
        have = self.order[: 2 - phase]
        for copy in self.arriving:
            copy.wait_recv()
        for a in range(len(self.grids)):
            for low, high, own, source in zip(
                self.target(phase, self.low, a),
                self.target(phase, self.high, a),
                self.target(phase, self.own, a),
                self.source(phase, a, self.at),
            ):
                shape = rect_shape(have, self.widths[a], self.rows[1])
                if "y" in have and "z" not in have:
                    shape = half_shape(have, shape)
                add_into(own, [own if phase == 0 else source, low, high], shape)

    def last(self):
        self.arriving = []
        for k, step in enumerate(STEPS):
            partner = moved(self.at, self.order[0], step)
            for a in range(len(self.grids)):
                self.arriving += self.push(
                    self.source(2, a, partner), [self.direct[a].at[k]], partner
                )

    def result(self, out, starts):
        for copy in self.arriving:
            copy.wait_recv()
        for a, start in enumerate(starts):
            (mine,) = self.source(2, a, self.at)
            total = mine[0, 0].astype(FULL)
            for k in range(3):
                total = total + self.direct[a][k, 0, 0].astype(FULL)
            out[pl.ds(*self.rows), start : start + self.widths[a]] = total


def hbm():
    return pl.BlockSpec(memory_space=pltpu.HBM)


def anywhere():
    return pl.BlockSpec(memory_space=pl.ANY)


def vmem():
    return pl.BlockSpec(memory_space=pltpu.VMEM)


def tail_kernel(grid, unit_behind, vector, out, totals, *rest):
    buffers = rest[:-8]
    whole, other, other_behind, line, near_lines, send, receive, local = rest[-8:]
    at = place()
    core = at["core"]
    sibling = moved(at, "core", 1)
    greet([sibling] + [moved(at, axis, step) for axis in ALL for step in STEPS])
    copies = Copies(send, receive)
    sent = []

    def send_line(phase):
        started = [
            copies.start(line.at[phase], near_lines.at[phase, k], moved(at, ALL[phase], step))
            for k, step in enumerate(STEPS)
        ]
        sent.extend(started)
        return started

    def add_line(phase, started):
        for copy in started:
            copy.wait_recv()
        parts = [line[phase]] + [near_lines[phase, k] for k in range(3)]
        line[phase + 1, 0:88, :] = (parts[0][:88] + parts[1][:88]) + (parts[2][:88] + parts[3][:88])
        line[phase + 1, 88:96, :] = jnp.maximum(
            jnp.maximum(parts[0][88:], parts[1][88:]), jnp.maximum(parts[2][88:], parts[3][88:])
        )

    line[0] = vector[...]
    mine = pl.ds(pl.multiple_of(core * 72, 8), 72)
    theirs = pl.ds(pl.multiple_of((1 - core) * 72, 8), 72)
    arriving = send_line(0)
    behind = copies.start(unit_behind.at[theirs], other_behind, sibling)
    sent.append(behind)
    local = [local, 0]
    scatters = []
    for part in PARTS:
        count = len(buffers) // 3
        k = len(scatters)
        scatters.append(
            Scatter(copies, at, [grid], WIDTHS[:1], part, buffers[k * count : (k + 1) * count], local)
        )
    for s in scatters:
        s.begin(0)
    add_line(0, arriving)
    arriving = send_line(1)
    for s in scatters:
        s.relay(0)
    add_line(1, arriving)
    arriving = send_line(2)
    for phase in (0, 1):
        for s in scatters:
            s.finish(phase)
            if phase == 0:
                s.begin(1)
            else:
                s.last()
        if phase == 0:
            add_line(2, arriving)
            last = copies.start(line.at[3], totals.at[core], sibling)
            sent.append(last)
            totals[core] = line[3]
            for s in scatters:
                s.relay(1)
    for s in scatters:
        s.result(whole, [0])
    swap = copies.start(whole.at[theirs], other, sibling)
    sent.append(swap)
    out[core, :, 0:256] = whole[mine, :]
    out[core, :, 256:UNIT] = unit_behind[mine, :]
    behind.wait_recv()
    out[1 - core, :, 256:UNIT] = other_behind[...]
    swap.wait_recv()
    out[1 - core, :, 0:256] = other[...]
    last.wait_recv()
    for copy in sent + [copy for s in scatters for copy in s.sent]:
        copy.wait_send()


def tail_scatter(grid, unit_behind, vector):
    shapes = []
    for part in PARTS:
        shapes += Scatter.shapes(WIDTHS[:1], part)
    count = 12 + 3 * 15
    return pl.pallas_call(
        tail_kernel,
        out_shape=[
            jax.ShapeDtypeStruct((2, 72, UNIT), FULL),
            jax.ShapeDtypeStruct((2, 96, 128), FULL),
        ],
        in_specs=[anywhere(), vmem(), vmem()],
        out_specs=[vmem()] * 2,
        scratch_shapes=shapes
        + [
            pltpu.VMEM((144, 256), FULL),
            pltpu.VMEM((72, 256), FULL),
            pltpu.VMEM((72, UNIT - 256), FULL),
            pltpu.VMEM((4, 96, 128), FULL),
            pltpu.VMEM((3, 3, 96, 128), FULL),
            pltpu.SemaphoreType.DMA((count,)),
            pltpu.SemaphoreType.DMA((count,)),
            pltpu.SemaphoreType.DMA((12,)),
        ],
        compiler_params=pltpu.CompilerParams(
            collective_id=1, has_side_effects=True, vmem_limit_bytes=24 << 20
        ),
        name="tail_scatter",
    )(grid, unit_behind, vector)


def swap_kernel(mine, theirs, send, receive):
    sibling = moved(place(), "core", 1)
    greet([sibling])
    Copies(send, receive).start(mine, theirs, sibling).wait()


def swap(mine, number):
    return pl.pallas_call(
        swap_kernel,
        out_shape=jax.ShapeDtypeStruct(mine.shape, mine.dtype),
        in_specs=[anywhere()],
        out_specs=anywhere(),
        scratch_shapes=[pltpu.SemaphoreType.DMA((1,)), pltpu.SemaphoreType.DMA((1,))],
        compiler_params=pltpu.CompilerParams(collective_id=number, has_side_effects=True),
        name=f"swap_{number}",
    )(mine)


def picker(which):
    row = lax.broadcasted_iota(jnp.int32, (256, 128), 0)
    lane = lax.broadcasted_iota(jnp.int32, (256, 128), 1)
    return jnp.where((row == lane + HEAD_DIM * which) & (lane < HEAD_DIM), 1.0, 0.0).astype(LOW)


def placer(which):
    row = lax.broadcasted_iota(jnp.int32, (128, 256), 0)
    lane = lax.broadcasted_iota(jnp.int32, (128, 256), 1)
    return jnp.where((lane == row + HEAD_DIM * which) & (row < HEAD_DIM), 1.0, 0.0).astype(LOW)


def dot(left, right):
    return jnp.dot(left, right, preferred_element_type=FULL)


def dot_rows(left, right):
    return lax.dot_general(left, right, (((0,), (0,)), ((), ())), preferred_element_type=FULL)


def dot_cols(left, right):
    return lax.dot_general(left, right, (((1,), (1,)), ((), ())), preferred_element_type=FULL)


def set_ids(ids, r, ids_row, ids_col):
    eye = lax.broadcasted_iota(jnp.int32, (128, 128), 0) == lax.broadcasted_iota(
        jnp.int32, (128, 128), 1
    )
    for k in range(8):
        piece = ids[k : k + 1, :]
        ids_row[r, :, k * 128 : (k + 1) * 128] = piece
        ids_col[r, k * 128 : (k + 1) * 128, :] = jnp.sum(
            jnp.where(eye, piece, 0.0), axis=1, keepdims=True
        )


def forward_kernel(
    pack, n1, cot, ids, bias, go, gu, gd, gq_out, rows_one, cot_rows, ids_other, mixed, qkv, logsum, peak,
    both, unit, gq, proj, ids_row, ids_col, q_s, k_s, v_s, out_s, top_s, send, receive, local,
):
    at = place()
    core, z = at["core"], at["z"]
    sibling = moved(at, "core", 1)
    partners = [moved(at, "z", step) for step in STEPS]
    greet([sibling] + [moved(at, axis, step) for axis in ALL for step in STEPS])
    copies = Copies(send, receive)
    mine = pl.ds(pl.multiple_of(core * 72, 8), 72)
    first = copies.start(pack.at[1 - core], both.at[mine], sibling)
    ids_copy = copies.start(ids, ids_other, sibling)
    n1_copy = copies.start(n1, rows_one.at[pl.ds(256, 256)], sibling)
    cot_copy = copies.start(cot, cot_rows.at[pl.ds(256, 256)], sibling)
    n1_own = pltpu.make_async_copy(n1, rows_one.at[pl.ds(0, 256)], local.at[0])
    cot_own = pltpu.make_async_copy(cot, cot_rows.at[pl.ds(0, 256)], local.at[1])
    n1_own.start()
    cot_own.start()
    both[mine, :] = pack[core]
    first.wait_recv()
    unit[...] = both[...].astype(LOW)
    block = (at["y"] // 2) * 4 + z
    gq[at["y"] % 2, at["x"], :, lanes(block * 256, 256)] = unit[:, 0:256]
    held = []
    for k, grid in enumerate((go, gu, gd)):
        (spot,) = spots(ALL, "", at, WIDTHS[k + 1], (0, 144))
        copy = pltpu.make_async_copy(
            unit.at[:, pl.ds(STARTS[k + 1], WIDTHS[k + 1])],
            grid.at[at["y"] % 2, at["x"], :, spot[3]],
            local.at[2 + k],
        )
        copy.start()
        held.append(copy)
    ahead = [Gather(copies, at, [gq], WIDTHS[:1], part) for part in PARTS]
    behind = [Gather(copies, at, [go, gu, gd], WIDTHS[1:], part) for part in PARTS_BEHIND]
    for g in ahead:
        g.first()
    for phase in (1, 2):
        for g in ahead:
            g.ring(phase)
        for g in ahead:
            g.forward(phase)
    for copy in held:
        copy.wait()
    for g in behind:
        g.first()
    n1_own.wait()
    n1_copy.wait_recv()
    ids_copy.wait_recv()
    set_ids(ids, 0, ids_row, ids_col)
    set_ids(ids_other, 1, ids_row, ids_col)
    for g in ahead:
        g.settle()
    started = []
    for step in STEPS + (0,):
        to = (z + step) % 4
        spot = lanes(to * 512, 512)
        weights = gq[:, :, :, spot].reshape(1152, 512)
        product = (dot(rows_one[...], weights) + bias[:, spot]).astype(LOW)
        if step:
            proj[to] = product
            started.append(copies.start(proj.at[to], qkv.at[z], moved(at, "z", step)))
        else:
            qkv[z] = product
        if step == 1:
            for g in behind:
                g.ring(1)
        if step == 2:
            for g in behind:
                g.forward(1)
    for g in behind:
        g.ring(2)
    gq_copy = pltpu.make_async_copy(gq, gq_out, local.at[5])
    gq_copy.start()
    for copy in started:
        copy.wait_recv()
    for r in range(2):
        for j in range(2):
            for b in range(4):
                block = qkv[b, r * 256 : (r + 1) * 256, j * 256 : (j + 1) * 256]
                spot = slice(b * 256, (b + 1) * 256)
                q_s[2 * r + j, spot, :] = dot(block, picker(0)).astype(LOW)
                k_s[2 * r + j, spot, :] = dot(block, picker(1)).astype(LOW)
                v_s[2 * r + j, spot, :] = dot(block, picker(2)).astype(LOW)
    top_s[...] = jnp.full(top_s.shape, LOWEST, FULL)
    back = []
    for step in STEPS + (0,):
        b = (z + step) % 4
        rows = pl.ds(pl.multiple_of(b * 256, 256), 256)

        @pl.loop(0, 4)
        def _(n, b=b, rows=rows):
            r, j = n // 2, n % 2
            scores = dot_cols(q_s[n, rows, :], k_s[n]) * SCALE
            query_ids = ids_col[r, rows, :]
            scores = jnp.where(query_ids == ids_row[r], scores, LOWEST)
            top = jnp.max(scores, axis=1, keepdims=True)
            expo = jnp.exp(scores - top)
            total = jnp.sum(expo, axis=1, keepdims=True)
            weights = (expo * (1.0 / total)).astype(LOW)
            out_s[n, b] = dot(weights, v_s[n]).astype(LOW)
            logsum[n, rows, :] = top + jnp.log(total)
            top_s[n] = jnp.maximum(top_s[n], jnp.where(query_ids >= 0.0, top, LOWEST))

        for n in range(4):
            r, j = n // 2, n % 2
            source = out_s.at[n, b]
            spot = (pl.ds(r * 256, 256), lanes(z * 256 + j * 128, 128))
            if step:
                back.append(copies.start(source, mixed.at[spot], moved(at, "z", step)))
            else:
                copy = pltpu.make_async_copy(source, mixed.at[spot], local.at[6 + n])
                copy.start()
                back.append(copy)
        if step == 2:
            for g in behind:
                g.forward(2)
    row = lax.broadcasted_iota(jnp.int32, (8, 128), 0)
    high = [jnp.maximum(jnp.max(top_s[j]), jnp.max(top_s[2 + j])) for j in range(2)]
    peak[...] = jnp.where(row == 0, high[0], high[1])
    for copy in back[:12]:
        copy.wait_recv()
    for copy in back[12:]:
        copy.wait()
    cot_own.wait()
    cot_copy.wait_recv()
    gq_copy.wait()
    for g in behind:
        g.settle()
    sent = [first, ids_copy, n1_copy, cot_copy] + started + back[:12]
    for copy in sent + [copy for g in ahead + behind for copy in g.sent]:
        copy.wait_send()


def forward(pack, n1, cot, ids, bias):
    count = 4 + 3 + 12 + 4 * 45
    return pl.pallas_call(
        forward_kernel,
        out_shape=[
            jax.ShapeDtypeStruct((2, 4, 144, 1024), LOW),
            jax.ShapeDtypeStruct((2, 4, 144, HIDDEN), LOW),
            jax.ShapeDtypeStruct((2, 4, 144, HIDDEN), LOW),
            jax.ShapeDtypeStruct((2, 4, 144, 2048), LOW),
            jax.ShapeDtypeStruct((512, 1152), LOW),
            jax.ShapeDtypeStruct((512, 1152), LOW),
            jax.ShapeDtypeStruct((8, 128), FULL),
            jax.ShapeDtypeStruct((512, 1024), LOW),
            jax.ShapeDtypeStruct((4, 512, 512), LOW),
            jax.ShapeDtypeStruct((4, 1024, 1), FULL),
            jax.ShapeDtypeStruct((8, 128), FULL),
        ],
        in_specs=[vmem(), anywhere(), anywhere(), vmem(), vmem()],
        out_specs=[hbm()] * 4
        + [vmem(), hbm(), vmem(), anywhere(), vmem(), vmem(), vmem()],
        scratch_shapes=[
            pltpu.VMEM((144, UNIT), FULL),
            pltpu.VMEM((144, UNIT), LOW),
            pltpu.VMEM((2, 4, 144, 2048), LOW),
            pltpu.VMEM((4, 512, 512), LOW),
            pltpu.VMEM((2, 1, 1024), FULL),
            pltpu.VMEM((2, 1024, 1), FULL),
        ]
        + [pltpu.VMEM((4, 1024, 128), LOW)] * 3
        + [
            pltpu.VMEM((4, 4, 256, 128), LOW),
            pltpu.VMEM((4, 256, 1), FULL),
            pltpu.SemaphoreType.DMA((count,)),
            pltpu.SemaphoreType.DMA((count,)),
            pltpu.SemaphoreType.DMA((10,)),
        ],
        compiler_params=pltpu.CompilerParams(
            collective_id=0, has_side_effects=True, vmem_limit_bytes=48 << 20
        ),
        name="forward_attention",
    )(pack, n1, cot, ids, bias)


def backward_kernel(
    upstream, qkv, ids, ids_other, logsum, go, gu, gd, back, unit, *rest
):
    (
        grad, q_s, k_s, v_s, g_s, dq_s, dk_s, dv_s, out_s, ids_row, ids_col, send, receive, local,
    ) = rest[:14]
    buffers = rest[14:]
    at = place()
    z = at["z"]
    partners = [moved(at, "z", step) for step in STEPS]
    greet([moved(at, axis, step) for axis in ALL for step in STEPS])
    copies = Copies(send, receive)
    started = [
        copies.start(upstream.at[:, lanes(partner["z"] * 256, 256)], grad.at[z], partner)
        for partner in partners
    ]
    own = pltpu.make_async_copy(upstream.at[:, lanes(z * 256, 256)], grad.at[z], local.at[0])
    own.start()
    counter = [local, 3]
    scatters = []
    for k, part in enumerate(PARTS_BEHIND):
        count = len(buffers) // 3
        scatters.append(
            Scatter(
                copies, at, [go, gu, gd], WIDTHS[1:], part, buffers[k * count : (k + 1) * count], counter
            )
        )
    for s in scatters:
        s.begin(0)
    set_ids(ids, 0, ids_row, ids_col)
    set_ids(ids_other, 1, ids_row, ids_col)
    for r in range(2):
        for j in range(2):
            for b in range(4):
                block = qkv[b, r * 256 : (r + 1) * 256, j * 256 : (j + 1) * 256]
                spot = slice(b * 256, (b + 1) * 256)
                q_s[2 * r + j, spot, :] = dot(block, picker(0)).astype(LOW)
                k_s[2 * r + j, spot, :] = dot(block, picker(1)).astype(LOW)
                v_s[2 * r + j, spot, :] = dot(block, picker(2)).astype(LOW)
    own.wait()
    for copy in started:
        copy.wait_recv()
    lane = lax.broadcasted_iota(jnp.int32, (256, 128), 1)
    for r in range(2):
        for j in range(2):
            for b in range(4):
                block = grad[b, r * 256 : (r + 1) * 256, j * 128 : (j + 1) * 128]
                g_s[2 * r + j, b * 256 : (b + 1) * 256, :] = jnp.where(
                    lane < HEAD_DIM, block.astype(FULL), 0.0
                ).astype(LOW)
    sent = []
    for r in range(2):
        for j in range(2):
            n = 2 * r + j
            dk_s[...] = jnp.zeros(dk_s.shape, FULL)
            dv_s[...] = jnp.zeros(dv_s.shape, FULL)

            @pl.loop(0, 4)
            def _(b, n=n, r=r):
                rows = pl.ds(pl.multiple_of(b * 256, 256), 256)
                query, upper = q_s[n, rows, :], g_s[n, rows, :]
                scores = dot_cols(query, k_s[n]) * SCALE
                allowed = ids_col[r, rows, :] == ids_row[r]
                probs = jnp.where(allowed, jnp.exp(scores - logsum[n, rows, :]), 0.0)
                dv_s[...] += dot_rows(probs.astype(LOW), upper)
                prob_grad = dot_cols(upper, v_s[n])
                centre = jnp.sum(probs * prob_grad, axis=1, keepdims=True)
                score_grad = (probs * (prob_grad - centre)).astype(LOW)
                dq_s[rows, :] = (dot(score_grad, k_s[n]) * SCALE).astype(LOW)
                dk_s[...] += dot_rows(score_grad, query)

            for b in range(4):
                spot = slice(b * 256, (b + 1) * 256)
                out_s[b, r * 256 : (r + 1) * 256, j * 256 : (j + 1) * 256] = (
                    dot(dq_s[spot, :], placer(0))
                    + dot((dk_s[spot, :] * SCALE).astype(LOW), placer(1))
                    + dot(dv_s[spot, :].astype(LOW), placer(2))
                ).astype(LOW)
            if n == 0:
                for s in scatters:
                    s.relay(0)
        rows = pl.ds(r * 256, 256)
        for partner in partners:
            source = out_s.at[partner["z"], rows]
            sent.append(copies.start(source, back.at[rows, lanes(z * 512, 512)], partner))
        copy = pltpu.make_async_copy(
            out_s.at[z, rows], back.at[rows, lanes(z * 512, 512)], local.at[1 + r]
        )
        copy.start()
        sent.append(copy)
    for s in scatters:
        s.finish(0)
        s.begin(1)
    for s in scatters:
        s.relay(1)
    for s in scatters:
        s.finish(1)
        s.last()
    for s in scatters:
        s.result(unit, [start - 256 for start in STARTS[1:]])
    for copy in sent:
        copy.wait()
    for copy in started + [copy for s in scatters for copy in s.sent]:
        copy.wait_send()


def backward(upstream, qkv, ids, ids_other, logsum, grids):
    count = 3 + 6 + 3 * 45
    shapes = []
    for part in PARTS_BEHIND:
        shapes += Scatter.shapes(WIDTHS[1:], part)
    return pl.pallas_call(
        backward_kernel,
        out_shape=[
            jax.ShapeDtypeStruct((512, 2048), LOW),
            jax.ShapeDtypeStruct((144, UNIT - 256), FULL),
        ],
        in_specs=[anywhere(), vmem(), vmem(), vmem(), vmem()] + [anywhere()] * 3,
        out_specs=[anywhere(), vmem()],
        scratch_shapes=[pltpu.VMEM((4, 512, 256), LOW)]
        + [pltpu.VMEM((4, 1024, 128), LOW)] * 4
        + [
            pltpu.VMEM((1024, 128), LOW),
            pltpu.VMEM((1024, 128), FULL),
            pltpu.VMEM((1024, 128), FULL),
            pltpu.VMEM((4, 512, 512), LOW),
            pltpu.VMEM((2, 1, 1024), FULL),
            pltpu.VMEM((2, 1024, 1), FULL),
            pltpu.SemaphoreType.DMA((count,)),
            pltpu.SemaphoreType.DMA((count,)),
            pltpu.SemaphoreType.DMA((48,)),
        ]
        + shapes,
        compiler_params=pltpu.CompilerParams(
            collective_id=3, has_side_effects=True, vmem_limit_bytes=52 << 20
        ),
        name="backward_attention",
    )(upstream, qkv, ids, ids_other, logsum, *grids)


def normalize(values, gain, shift):
    centre = values - jnp.mean(values, axis=-1, keepdims=True)
    inverse = lax.rsqrt(jnp.mean(centre * centre, axis=-1, keepdims=True) + EPSILON)
    scaled = centre * inverse
    return (scaled * gain + shift, scaled, inverse)


def normalize_back(upstream, scaled, inverse, gain):
    along = upstream * gain
    width_mean = jnp.mean(along, axis=-1, keepdims=True)
    cross_mean = jnp.mean(along * scaled, axis=-1, keepdims=True)
    return inverse * (along - width_mean - scaled * cross_mean)


def smooth(inner):
    return jax.nn.gelu(inner, approximate=True)


def selector(offset):
    matrix = np.zeros((1024, 128), np.float32)
    for t in range(8):
        for i in range(TAIL):
            matrix[128 * t + offset + i, TAIL * t + i] = 1.0
    return jnp.asarray(matrix, LOW)


def per_device(
    tokens,
    picture,
    cotangent,
    gain_one,
    shift_one,
    query_weight,
    query_bias,
    key_weight,
    value_weight,
    value_bias,
    out_weight,
    out_bias,
    gain_two,
    shift_two,
    up_weight,
    up_bias,
    down_weight,
    down_bias,
):
    width = tokens.shape[1]
    t = lax.axis_index("tensor")
    core = lax.axis_index("dp") % 2
    z = t % 4
    gain_first = gain_one.astype(FULL)
    gain_second = gain_two.astype(FULL)

    out_t = out_weight.astype(FULL).T
    down_t = down_weight.astype(FULL).T
    up = up_weight.astype(FULL)
    halves = []
    for h in range(2):
        cols = slice(h * 72, (h + 1) * 72)
        first = h * (MAIN + TAIL)
        main, tail = slice(first, first + MAIN), slice(first + MAIN, first + MAIN + TAIL)
        halves.append(
            jnp.concatenate(
                [
                    query_weight[:, cols].astype(FULL),
                    key_weight[:, cols].astype(FULL),
                    value_weight[:, cols].astype(FULL),
                    jnp.zeros((72, 40), FULL),
                    out_t[:, cols],
                    up[:, tail],
                    down_t[:, tail],
                    jnp.zeros((72, 30), FULL),
                    up[:, main],
                    down_t[:, main],
                ],
                axis=1,
            )
        )
    pack = jnp.stack(halves)

    inputs = tokens.astype(FULL)
    normed, scaled_one, inverse_one = normalize(inputs, gain_first, shift_one.astype(FULL))
    normed_mine = normed.astype(LOW)
    half = lax.dynamic_slice_in_dim(picture, (t // 4) * 1024, 1024)
    ids = jnp.where(half >= 0, half, -1 - jnp.arange(1024, dtype=jnp.int32)).astype(FULL)
    def halves_of(vector, size):
        return lax.dynamic_index_in_dim(
            vector.astype(FULL).reshape(8, 2, size), core, axis=1, keepdims=False
        )

    query_b, value_b = halves_of(query_bias, 72), halves_of(value_bias, 72)
    proj_bias = jnp.concatenate(
        [query_b, jnp.zeros((8, 72), FULL), value_b, jnp.zeros((8, 40), FULL)], axis=1
    ).reshape(1, 2048)
    up_b = halves_of(up_bias, MAIN + TAIL)
    hidden_bias = jnp.concatenate(
        [up_b[:, :MAIN].reshape(2048), up_b[:, MAIN:].reshape(8 * TAIL), jnp.zeros((24,), FULL)]
    )

    go, gu, gd, gq, rows_one, cot_rows, ids_other, mixed, qkv, logsum, peak = forward(
        pack, normed_mine, cotangent, ids.reshape(8, 128), proj_bias
    )
    gq, go = gq.reshape(width, 2048), go.reshape(width, 1024)
    select_up, select_down = selector(72), selector(72 + TAIL)
    gu = lax.dynamic_update_slice(
        gu.reshape(width, HIDDEN), dot(go, select_up).astype(LOW), (0, 2048)
    )
    gd = lax.dynamic_update_slice(
        gd.reshape(width, HIDDEN), dot(go, select_down).astype(LOW), (0, 2048)
    )
    part = dot_cols(mixed, go)
    branch = part[:256] + swap(part[256:].astype(LOW), 4).astype(FULL) + out_bias.astype(FULL)
    middle = inputs + branch
    normed_two, scaled_two, inverse_two = normalize(middle, gain_second, shift_two.astype(FULL))
    normed_two = normed_two.astype(LOW)
    rows_two = jnp.concatenate([normed_two, swap(normed_two, 5)])
    hidden = dot(rows_two, gu) + hidden_bias
    active = smooth(hidden).astype(LOW)
    part = dot_cols(active, gd)
    result = middle + (
        part[:256] + swap(part[256:].astype(LOW), 6).astype(FULL) + down_bias.astype(FULL)
    )

    upstream = cotangent.astype(FULL)
    active_grad = dot(cot_rows, gd)
    _, gelu_back = jax.vjp(smooth, hidden)
    hidden_grad = gelu_back(active_grad)[0].astype(LOW)
    part = dot_cols(hidden_grad, gu)
    normed_two_grad = part[:256] + swap(part[256:].astype(LOW), 7).astype(FULL)
    middle_grad = upstream + normalize_back(normed_two_grad, scaled_two, inverse_two, gain_second)
    branch_low = middle_grad.astype(LOW)
    branch_rows = jnp.concatenate([branch_low, swap(branch_low, 8)])
    mixed_grad = dot(branch_rows, go).astype(LOW)

    shape = (2, 4, 144)
    grad_u = dot_rows(rows_two, hidden_grad[:, :2048]).astype(LOW)
    grad_d = dot_rows(cot_rows, active[:, :2048]).astype(LOW)
    up_tail = dot_cols(hidden_grad[:, 2048:], select_up).astype(LOW)
    down_tail = dot_cols(active[:, 2048:], select_down).astype(LOW)
    grad_o = dot_rows(
        jnp.concatenate([branch_rows, rows_two, cot_rows]),
        jnp.concatenate([mixed, up_tail, down_tail]),
    ).astype(LOW)
    proj_grad, unit_behind = backward(
        mixed_grad,
        qkv,
        ids.reshape(8, 128),
        ids_other,
        logsum,
        [
            grad_o.reshape(shape + (1024,)),
            grad_u.reshape(shape + (2048,)),
            grad_d.reshape(shape + (2048,)),
        ],
    )
    part = dot_cols(proj_grad, gq)
    normed_one_grad = part[:256] + swap(part[256:].astype(LOW), 9).astype(FULL)
    input_grad = middle_grad + normalize_back(normed_one_grad, scaled_one, inverse_one, gain_first)

    grad_q = dot_rows(rows_one, proj_grad).astype(LOW)

    head = lax.broadcasted_iota(jnp.int32, (8, 128), 1)
    peaks = jnp.where(
        head == 4 * z + core,
        peak[0, 0],
        jnp.where(head == 4 * z + 2 + core, peak[1, 0], LOWEST),
    )

    def total(values):
        return jnp.sum(values.astype(FULL), axis=0)

    vector = jnp.concatenate(
        [
            total(proj_grad),
            total(hidden_grad),
            total(branch_low),
            total(upstream),
            total(normed_one_grad * scaled_one),
            total(normed_one_grad),
            total(normed_two_grad * scaled_two),
            total(normed_two_grad),
            jnp.zeros((128,), FULL),
        ]
    ).reshape(88, 128)
    vector = jnp.concatenate([vector, peaks])
    grads, totals = tail_scatter(grad_q.reshape(shape + (2048,)), unit_behind, vector)

    def side(first, size):
        return jnp.concatenate([grads[0, :, first : first + size], grads[1, :, first : first + size]], axis=1)

    def hidden_side(main, tail):
        return jnp.concatenate(
            [
                grads[0, :, main : main + MAIN],
                grads[0, :, tail : tail + TAIL],
                grads[1, :, main : main + MAIN],
                grads[1, :, tail : tail + TAIL],
            ],
            axis=1,
        )

    query_w, key_w, value_w = side(0, 72), side(72, 72), side(144, 72)
    out_w = side(256, 72).T
    up_w = hidden_side(384, 256 + 72)
    down_w = hidden_side(640, 256 + 72 + TAIL).T
    flat = totals[:, :88].reshape(2, 88 * 128)
    heads = flat[:, :2048].reshape(2, 8, 256)
    query_b_grad = heads[:, :, :72].transpose(1, 0, 2).reshape(width)
    value_b_grad = heads[:, :, 144:216].transpose(1, 0, 2).reshape(width)
    up_b_grad = (
        jnp.concatenate(
            [
                flat[:, 2048:4096].reshape(2, 8, MAIN),
                flat[:, 4096 : 4096 + 8 * TAIL].reshape(2, 8, TAIL),
            ],
            axis=2,
        )
        .transpose(1, 0, 2)
        .reshape(-1)
    )
    summed = (flat[0] + flat[1])[2048 + HIDDEN : 2048 + HIDDEN + 6 * width].reshape(6, width)
    high = jnp.maximum(totals[0, 88, :16], totals[1, 88, :16])
    factor = jnp.sqrt(CLIP_LIMIT / jnp.maximum(high, CLIP_LIMIT))
    column_factor = jnp.repeat(lax.dynamic_slice_in_dim(factor, 2 * t, 2), HEAD_DIM)
    clipped_query = query_weight.astype(FULL) * column_factor[None, :]
    clipped_key = key_weight.astype(FULL) * column_factor[None, :]
    return (
        result,
        input_grad,
        query_w,
        key_w,
        value_w,
        out_w,
        up_w,
        down_w,
        query_b_grad,
        value_b_grad,
        up_b_grad,
        summed[0],
        summed[1],
        summed[2],
        summed[3],
        summed[4],
        summed[5],
        clipped_query,
        clipped_key,
    )


def solution(mesh):
    in_specs = (
        P(("dp", "tensor"), None),
        P("dp"),
        P(("dp", "tensor"), None),
        P(),
        P(),
        P("dp", "tensor"),
        P(),
        P("dp", "tensor"),
        P("dp", "tensor"),
        P(),
        P("tensor", "dp"),
        P(),
        P(),
        P(),
        P("dp", "tensor"),
        P(),
        P("tensor", "dp"),
        P(),
    )
    out_specs = (
        P(("dp", "tensor"), None),
        P(("dp", "tensor"), None),
        P("dp", "tensor"),
        P("dp", "tensor"),
        P("dp", "tensor"),
        P("tensor", "dp"),
        P("dp", "tensor"),
        P("tensor", "dp"),
        P(),
        P(),
        P(),
        P(),
        P(),
        P(),
        P(),
        P(),
        P(),
        P("dp", "tensor"),
        P("dp", "tensor"),
    )
    return jax.shard_map(
        per_device, mesh=mesh, in_specs=in_specs, out_specs=out_specs, check_vma=False
    )
```

time: 461 us -> 381 us (0.83)
  Pallas kernels: 317 us -> 237 us
  matrix products: 72.1 us -> 77.3 us
    pallas_call x4 -> x3, Pallas kernels: 299 us -> 212 us  [the longest x1 98.6 us: forward(): pl.pallas_call(forward_kernel, out_shape=[jax.ShapeDtypeStruct((2, 4, 144...]
    unnamed x133 -> x131, local copies, waits for them, and re-layouts: 22.2 us -> 14.2 us
    pallas_call x6, Pallas kernels: 18.1 us -> 25.4 us  [swap(): pl.pallas_call(swap_kernel, out_shape=jax.ShapeDtypeStruct(mine.shape, mi...]
    dot_general x6 -> x5, matrix products: 33.5 us -> 37.4 us  [dot(): return jnp.dot(left, right, preferred_element_type=FULL)]
where the time goes in v2:
time: 381 us; the launch traced here: 377 us
  Pallas kernels  237 us (62%)
  matrix products  77.3 us (20%)
  other arithmetic  30.1 us (8%)
  local copies, waits for them, and re-layouts  30.1 us (8%)
    pallas_call x1, Pallas kernels, forward(): pl.pallas_call(forward_kernel, out_shape=[jax.ShapeDtypeStruct((2, 4, 144...  98.6 us
    pallas_call x1, Pallas kernels, backward(): pl.pallas_call(backward_kernel, out_shape=[jax.ShapeDtypeStruct((512, 204...  74.6 us
    pallas_call x1, Pallas kernels, tail_scatter(): pl.pallas_call(tail_kernel, out_shape=[jax.ShapeDtypeStruct((2, 72, UNIT)...  38.5 us
    dot_general x5, matrix products, dot(): return jnp.dot(left, right, preferred_element_type=FULL)  37.4 us
    pallas_call x6, Pallas kernels, swap(): pl.pallas_call(swap_kernel, out_shape=jax.ShapeDtypeStruct(mine.shape, mi...  25.4 us
    dot_general x6, matrix products, dot_cols(): lax.dot_general(left, right, (((1,), (1,)), ((), ())), preferred_element_...  21.5 us
    dot_general x4, matrix products, dot_rows(): lax.dot_general(left, right, (((0,), (0,)), ((), ())), preferred_element_...  18.4 us
    unnamed x131, local copies, waits for them, and re-layouts  14.2 us

profile of v2, /device:TPU:1, one launch (start us, length us, event | category | flops | bytes accessed | tf_op | source)
XLA Modules:
  0.0 376.6 jit_solution(17623604914835118011)
XLA Ops:
  9.4 98.6 %forward_attention.1 = (bf16[2,4,144,1024]{3,2,1,0:T(8,128)(2,1)}, bf16[2,4,144,2176]{3,2,1,0:T(8,128)(2,1)}, bf16[2,4,144,2176]{3,2,1,0:T(8,128)(2,1)}, bf16[2,...) custom-call(f32[2,72,896]{2,1,0:T(8,128)S(1)} %pad_maximum_fusion.3., ...), custom_call_target="tpu_custom_call" | custom-call | tf_op jit(solution)/shard_map/forward_attention/pallas_call | solution.py:626
  108.0 4.0 %fusion.56 = f32[512,1152]{1,0:T(8,128)S(1)} fusion(bf16[512,1024]{1,0:T(8,128)(2,1)S(1)} %get-tuple-element.34, bf16[1152,1024]{1,0:T(8,128)(2,1)} %bitcast.139), kind=kOutput, calls=%fused_computation.172 | convolution fusion | flops 1207959552 | bytes 5767168 | tf_op jit(solution)/shard_map/dot_general | solution.py:474
  114.4 9.5 %swap_4.1 = bf16[256,1152]{1,0:T(8,128)(2,1)} custom-call(bf16[256,1152]{1,0:T(8,128)(2,1)} %slice.419.mine), custom_call_target="tpu_custom_call" | custom-call | tf_op jit(solution)/shard_map/swap_4/pallas_call | solution.py:442
  128.2 18.5 %fusion.58 = f32[512,2176]{1,0:T(8,128)} fusion(bf16[512,1152]{1,0:T(8,128)(2,1)S(1)} %get-tuple-element.38, bf16[1152,2176]{1,0:T(8,128)(2,1)} %fusion.12), kind=kOutput, calls=%fused_computation.174 | convolution fusion | flops 2566914048 | bytes 10649600 | tf_op jit(solution)/shard_map/dot_general | solution.py:466
  153.3 3.2 fusion.13
  158.8 2.4 swap_5.1
  161.2 10.5 %convert_reduce_fusion = (f32[2176]{0:T(1024)}, bf16[512,2176]{1,0:T(8,128)(2,1)S(1)}, bf16[512,2176]{1,0:T(8,128)(2,1)}) fusion(f32[512,2176]{1,0:T(8,128)} %fusion.58, f32[2176]{0:T(1024)} %concatenate.56, bf16[1152,2176]{1,0:T(8,128)(2,1)} %fusion.13, bf16[256,1152]{1,0:T(8,128)(2,1)} %swap_5.1, bf16[256,1152]{1,0:T(8,128)(2,1)} %add_convert_fusion.mine), kind=kOutput, calls=%fused_computation.13 | convolution fusion | flops 2597124096 | bytes 15123456 | tf_op jit(solution)/shard_map/dot_general | solution.py:466
  171.7 6.5 %fusion.59 = f32[512,1152]{1,0:T(8,128)S(1)} fusion(bf16[512,2176]{1,0:T(8,128)(2,1)S(1)} %get-tuple-element.118, bf16[1152,2176]{1,0:T(8,128)(2,1)} %fusion.13), kind=kOutput, calls=%fused_computation.175 | convolution fusion | flops 2566914048 | bytes 9601024 | tf_op jit(solution)/shard_map/dot_general | solution.py:474
  180.5 2.4 swap_7.1
  182.9 2.8 multiply_reduce_fusion
  187.5 5.6 %fusion.57 = f32[512,1152]{1,0:T(8,128)S(1)} fusion(bf16[512,2176]{1,0:T(8,128)(2,1)S(1)} %copy-done.41, bf16[1152,2176]{1,0:T(8,128)(2,1)} %fusion.12), kind=kOutput, calls=%fused_computation.173 | convolution fusion | flops 2566914048 | bytes 9601024 | tf_op jit(solution)/shard_map/dot_general | solution.py:474
  195.4 2.4 swap_6.1
  197.8 5.1 %convert_reduce_fusion.4 = (f32[1152]{0:T(1024)}, bf16[256,1152]{1,0:T(8,128)(2,1)}, f32[256,1152]{1,0:T(8,128)}, f32[256,1152]{1,0:T(8,128)}, f32[1152]{0:T(1024)}) fusion(f32[256]{0:T(256)} %broadcast_multiply_fusion.2, f32[256,1152]{1,0:T(8,128)S(1)} %get-tuple-element.120, f32[256]{0:T(256)S(1)} %broadcast_multiply_fusion.4, ...), kind=kLoop, calls=%fused_computation.66 | loop fusion | flops 5601024 | bytes 8280064 | tf_op jit(solution)/shard_map/reduce_sum | solution.py:976
  202.9 2.4 swap_8.1
  205.2 3.6 convolution_convert_fusion.8.upstream
  212.8 5.2 %convolution_convert_fusion.3 = bf16[1152,1024]{1,0:T(8,128)(2,1)} fusion(bf16[1536,1152]{1,0:T(8,128)(2,1)S(1)} %constant_dynamic-update-slice_fusion, bf16[512,1024]{1,0:T(8,128)(2,1)S(1)} %convolution_convert_fusion.6, bf16[512,1024]{1,0:T(8,128)(2,1)S(1)} %convolution_convert_fusion.7, bf16[512,1024]{1,0:T(8,128)(2,1)S(1)} %copy-done.5), kind=kOutput, calls=%fused_computation.16 | convolution fusion | flops 3634495488 | bytes 9043968 | tf_op jit(solution)/shard_map/dot_general | solution.py:470
  218.0 4.3 %convolution_convert_fusion.2 = bf16[1152,2048]{1,0:T(8,128)(2,1)} fusion(bf16[512,2176]{1,0:T(8,128)(2,1)S(1)} %copy-done.44, bf16[256,1152]{1,0:T(8,128)(2,1)S(1)} %copy-done.12, bf16[256,1152]{1,0:T(8,128)(2,1)S(1)} %copy-done.14), kind=kOutput, calls=%fused_computation.2 | convolution fusion | flops 2420637696 | bytes 7995392 | tf_op jit(solution)/shard_map/dot_general | solution.py:470
  222.3 4.7 %convolution_convert_fusion.1 = bf16[1152,2048]{1,0:T(8,128)(2,1)} fusion(bf16[512,1152]{1,0:T(8,128)(2,1)S(1)} %get-tuple-element.38, bf16[512,2176]{1,0:T(8,128)(2,1)S(1)} %copy-done.42), kind=kOutput, calls=%fused_computation.1 | convolution fusion | flops 2418278400 | bytes 7995392 | tf_op jit(solution)/shard_map/dot_general | solution.py:470
  227.0 74.6 %backward_attention.1 = (bf16[512,2048]{1,0:T(8,128)(2,1)}, f32[144,640]{1,0:T(8,128)S(1)}) custom-call(bf16[512,1024]{1,0:T(8,128)(2,1)S(1)} %convolution_convert_fusion.8.upstream, bf16[4,512,512]{2,1,0:T(8,128)(2,1)} %get-tuple-element.39.qkv, f32[8,128]{1,0:T(8,128)S(1)} %fusion.39.ids, f32[8,128]{1,0:T(8,128)S(1)} %get-tuple-element.40.ids_other, ...), custom_call_target="tpu_custom_call" | custom-call | tf_op jit(solution)/shard_map/backward_attention/pallas_call | solution.py:778
  301.6 4.5 %fusion.60 = f32[512,1152]{1,0:T(8,128)S(1)} fusion(bf16[512,2048]{1,0:T(8,128)(2,1)} %get-tuple-element.42, bf16[1152,2048]{1,0:T(8,128)(2,1)S(1)} %bitcast.138), kind=kOutput, calls=%fused_computation.176 | convolution fusion | flops 2415919104 | bytes 9175040 | tf_op jit(solution)/shard_map/dot_general | solution.py:474
  308.4 6.5 %swap_9.1 = bf16[256,1152]{1,0:T(8,128)(2,1)} custom-call(bf16[256,1152]{1,0:T(8,128)(2,1)} %slice.416.mine), custom_call_target="tpu_custom_call" | custom-call | tf_op jit(solution)/shard_map/swap_9/pallas_call | solution.py:442
  317.1 2.9 fusion.27
  320.1 4.3 %convolution_convert_fusion = bf16[1152,2048]{1,0:T(8,128)(2,1)} fusion(bf16[512,1152]{1,0:T(8,128)(2,1)S(1)} %copy-done.3, bf16[512,2048]{1,0:T(8,128)(2,1)S(1)} %copy-done.15), kind=kOutput, calls=%fused_computation | convolution fusion | flops 2418278400 | bytes 7995392 | tf_op jit(solution)/shard_map/dot_general | solution.py:470
  329.2 38.5 %tail_scatter.1 = (f32[2,72,896]{2,1,0:T(8,128)S(1)}, f32[2,96,128]{2,1,0:T(8,128)S(1)}) custom-call(bf16[2,4,144,2048]{3,2,1,0:T(8,128)(2,1)S(1)} %bitcast.117, f32[144,640]{1,0:T(8,128)S(1)} %get-tuple-element.45.unit_behind, f32[96,128]{1,0:T(8,128)S(1)} %pad_maximum_fusion.8.vector), custom_call_target="tpu_custom_call" | custom-call | tf_op jit(solution)/shard_map/tail_scatter/pallas_call | solution.py:409
  (221 shorter events, 51.8 us)
Async XLA Ops:
  2.9 5.0 %copy-start.45 = (bf16[1152]{0:T(1024)(128)(2,1)S(1)}, bf16[1152]{0:T(1024)(128)(2,1)}, u32[]{:S(2)}) copy-start(bf16[1152]{0:T(1024)(128)(2,1)} %param.24) | copy-start | bytes 6916
  2.9 5.0 %copy-start.46 = (bf16[1152]{0:T(1024)(128)(2,1)S(1)}, bf16[1152]{0:T(1024)(128)(2,1)}, u32[]{:S(2)}) copy-start(bf16[1152]{0:T(1024)(128)(2,1)} %param.23) | copy-start | bytes 6916
  2.9 5.0 %copy-start.6 = (bf16[256,1152]{1,0:T(8,128)(2,1)S(1)}, bf16[256,1152]{1,0:T(8,128)(2,1)}, u32[]{:S(2)}) copy-start(bf16[256,1152]{1,0:T(8,128)(2,1)} %param.20) | copy-start | bytes 1769476
  108.0 4.1 %copy-start.2 = (bf16[512,1152]{1,0:T(8,128)(2,1)}, bf16[512,1152]{1,0:T(8,128)(2,1)S(1)}, u32[]{:S(2)}) copy-start(bf16[512,1152]{1,0:T(8,128)(2,1)S(1)} %get-tuple-element.44) | copy-start | bytes 3538948
  108.0 4.1 %copy-start.4 = (bf16[512,1024]{1,0:T(8,128)(2,1)}, bf16[512,1024]{1,0:T(8,128)(2,1)S(1)}, u32[]{:S(2)}) copy-start(bf16[512,1024]{1,0:T(8,128)(2,1)S(1)} %get-tuple-element.34) | copy-start | bytes 3145732
  153.3 3.2 copy-start.49
  153.3 3.2 copy-start.50
  153.3 4.4 %copy-start.34 = (f32[256]{0:T(256)S(1)}, f32[256]{0:T(256)}, u32[]{:S(2)}) copy-start(f32[256]{0:T(256)} %add_rsqrt_fusion) | copy-start | bytes 3076
  171.7 6.5 %copy-start.43 = (bf16[512,2176]{1,0:T(8,128)(2,1)}, bf16[512,2176]{1,0:T(8,128)(2,1)S(1)}, u32[]{:S(2)}) copy-start(bf16[512,2176]{1,0:T(8,128)(2,1)S(1)} %get-tuple-element.118) | copy-start | bytes 6684676
  182.9 4.0 %copy-start.51 = (bf16[1152]{0:T(1024)(128)(2,1)S(1)}, bf16[1152]{0:T(1024)(128)(2,1)}, u32[]{:S(2)}) copy-start(bf16[1152]{0:T(1024)(128)(2,1)} %param.37) | copy-start | bytes 6916
  182.9 4.6 %copy-start.41 = (bf16[512,2176]{1,0:T(8,128)(2,1)S(1)}, bf16[512,2176]{1,0:T(8,128)(2,1)}, u32[]{:S(2)}) copy-start(bf16[512,2176]{1,0:T(8,128)(2,1)} %get-tuple-element.121) | copy-start | bytes 6684676
  205.2 3.7 copy-start.7
  205.2 3.8 copy-start.13
  212.8 5.2 %copy-start.14 = (bf16[256,1152]{1,0:T(8,128)(2,1)S(1)}, bf16[256,1152]{1,0:T(8,128)(2,1)}, u32[]{:S(2)}) copy-start(bf16[256,1152]{1,0:T(8,128)(2,1)} %add_convert_fusion.mine) | copy-start | bytes 1769476
  222.3 79.3 %slice-start = ((s8[4718592]{0:T(1024)(128)(4,1)}), s8[4194304]{0:T(1024)(128)(4,1)S(1)}, s32[]{:S(2)}) async-start(s8[4718592]{0:T(1024)(128)(4,1)} %bitcast.136), calls=%async_computation | async-start | bytes 8388608
  227.0 74.7 %slice-start.1 = ((s8[4718592]{0:T(1024)(128)(4,1)}), s8[524288]{0:T(1024)(128)(4,1)S(1)}, s32[]{:S(2)}) async-start(s8[4718592]{0:T(1024)(128)(4,1)} %bitcast.136), calls=%async_computation.1 | async-start | bytes 1048576
  307.5 7.3 %copy-start.27 = (f32[1152]{0:T(1024)S(1)}, f32[1152]{0:T(1024)}, u32[]{:S(2)}) copy-start(f32[1152]{0:T(1024)} %copy-done.26) | copy-start | bytes 13828
  307.5 7.3 %copy-start.37 = (f32[256]{0:T(256)S(1)}, f32[256]{0:T(256)}, u32[]{:S(2)}) copy-start(f32[256]{0:T(256)} %copy-done.36) | copy-start | bytes 3076
  307.5 7.4 %copy-start.39 = (f32[256]{0:T(256)S(1)}, f32[256]{0:T(256)}, u32[]{:S(2)}) copy-start(f32[256]{0:T(256)} %copy-done.38) | copy-start | bytes 3076
  307.5 9.5 %copy-start.9 = (f32[256,1152]{1,0:T(8,128)S(1)}, f32[256,1152]{1,0:T(8,128)}, u32[]{:S(2)}) copy-start(f32[256,1152]{1,0:T(8,128)} %get-tuple-element.116) | copy-start | bytes 3538948
  317.1 3.0 copy-start.3
  320.1 6.2 %copy-start.16 = (bf16[512,2048]{1,0:T(8,128)(2,1)S(1)}, bf16[512,2048]{1,0:T(8,128)(2,1)}, u32[]{:S(2)}) copy-start(bf16[512,2048]{1,0:T(8,128)(2,1)} %get-tuple-element.42) | copy-start | bytes 6291460
  367.7 8.0 %copy-start.24 = (bf16[72,144]{1,0:T(8,128)(2,1)S(1)}, bf16[72,144]{1,0:T(8,128)(2,1)}, u32[]{:S(2)}) copy-start(bf16[72,144]{1,0:T(8,128)(2,1)} %param.25) | copy-start | bytes 62212
  367.7 8.0 %copy-start.25 = (bf16[72,144]{1,0:T(8,128)(2,1)S(1)}, bf16[72,144]{1,0:T(8,128)(2,1)}, u32[]{:S(2)}) copy-start(bf16[72,144]{1,0:T(8,128)(2,1)} %param.27) | copy-start | bytes 62212
  (32 other events, 53.6 us)
